TPU v7x, 128 devices: a whole 4x4x4 slice. The times are simulated.
128 devices in a mesh: batch: 4 (over z), seq: 32 (over y, x, core).
Axes of the slice: x: 4, y: 4, z: 4, core: 2. Of those that a mesh axis runs over, the one named last changes fastest.
Arguments:
- tokens: bfloat16 [2, 4, 4096, 576], P(None, 'batch', 'seq'), may hold values from -6 to 6
- doc_lengths: int32 [2, 4, 3], P(None, 'batch'), may hold values from 1 to 4094, as said below
- first_gain: bfloat16 [576], P('seq'), may hold values from 0.5 to 1.5
- query_weight: bfloat16 [576, 576], P('batch', 'seq'), may hold values from -0.25 to 0.25
- key_matrix: bfloat16 [576, 192], P('batch', 'seq'), may hold values from -0.25 to 0.25
- value_matrix: bfloat16 [576, 192], P('batch', 'seq'), may hold values from -0.25 to 0.25
- output_weight: bfloat16 [576, 576], P('batch', 'seq'), may hold values from -4 to 4
- second_gain: bfloat16 [576], P('seq'), may hold values from 0.5 to 1.5
- gate_weight: bfloat16 [576, 1536], P('batch', 'seq'), may hold values from -0.25 to 0.25
- up_weight: bfloat16 [576, 1536], P('batch', 'seq'), may hold values from -0.25 to 0.25
- down_weight: bfloat16 [1536, 576], P('batch', 'seq'), may hold values from -0.15625 to 0.15625
- cotangent: bfloat16 [2, 4, 4096, 576], P(None, 'batch', 'seq'), may hold values from -6 to 6
Outputs:
- mixed: bfloat16 [2, 4, 4096, 576], P(None, 'batch', 'seq')
- tokens_grad: bfloat16 [2, 4, 4096, 576], P(None, 'batch', 'seq')
- first_gain_grad: float32 [576], P('seq')
- query_grad: float32 [576, 576], P('batch', 'seq')
- key_grad: float32 [576, 192], P('batch', 'seq')
- value_grad: float32 [576, 192], P('batch', 'seq')
- output_grad: float32 [576, 576], P('batch', 'seq')
- second_gain_grad: float32 [576], P('seq')
- gate_grad: float32 [576, 1536], P('batch', 'seq')
- up_grad: float32 [576, 1536], P('batch', 'seq')
- down_grad: float32 [1536, 576], P('batch', 'seq')
Inputs may be any that keep to these rules, and one draw needn't show every extreme that they name: `doc_lengths`: in each row the 3 lengths sum to 4096; all but one of them, whose place in the row varies, are under 128 // 2. Some row holds the longest document possible.
All inputs are finite; a program needn't handle non-finite values.
Results may differ from a plain program's by a relative error of at most 0.028.
Values may be sent and summed in bfloat16 or wider, within the bound.
A program may use at most 128 MiB of HBM per device.

v0:
```python
import math

import jax
import jax.numpy as jnp
from jax import lax
from jax.sharding import PartitionSpec as P

MODEL_WIDTH = 576
QUERY_HEADS = 9
KEY_VALUE_HEADS = 3
HEAD_SIZE = 64
FF = 1536


EPS = 1e-05
THETA = 100000.0
MASKED = -1e30


def fetch(shards):
    tall = (
        lax.all_gather(shards[0], "batch", axis=0, tiled=True),
        lax.all_gather(shards[1], "batch", axis=0, tiled=True),
        lax.all_gather(shards[2], "batch", axis=0, tiled=True),
        lax.all_gather(shards[3], "batch", axis=0, tiled=True),
        lax.all_gather(shards[4], "batch", axis=0, tiled=True),
        lax.all_gather(shards[5], "batch", axis=0, tiled=True),
        lax.all_gather(shards[6], "batch", axis=0, tiled=True),
    )
    return (
        lax.all_gather(tall[0], "seq", axis=1, tiled=True),
        lax.all_gather(tall[1], "seq", axis=1, tiled=True),
        lax.all_gather(tall[2], "seq", axis=1, tiled=True),
        lax.all_gather(tall[3], "seq", axis=1, tiled=True),
        lax.all_gather(tall[4], "seq", axis=1, tiled=True),
        lax.all_gather(tall[5], "seq", axis=1, tiled=True),
        lax.all_gather(tall[6], "seq", axis=1, tiled=True),
        lax.all_gather(shards[7], "seq", axis=0, tiled=True),
        lax.all_gather(shards[8], "seq", axis=0, tiled=True),
    )


def doc_tables(lengths, total_count):
    ends = jnp.cumsum(lengths, axis=-1)
    starts = ends - lengths
    places = jnp.arange(total_count, dtype=jnp.int32)
    docs = jnp.sum((places[:, None] >= ends[..., None, :]).astype(jnp.int32), axis=-1)
    labels = jnp.arange(lengths.shape[-1], dtype=jnp.int32)
    first = jnp.sum(jnp.where(docs[..., None] == labels, starts[..., None, :], 0), axis=-1)
    return (docs, places - first)


def rope_tables(positions, width):
    half = width // 2
    inverse_rates = THETA ** (-2.0 * jnp.arange(half, dtype=jnp.float32) / width)
    angles = positions.astype(jnp.float32)[..., None] * inverse_rates
    angles = jnp.concatenate([angles, angles], axis=-1)
    return (jnp.cos(angles), jnp.sin(angles))


def apply_rotation(values, cosine_table, sine_table):
    half = values.shape[-1] // 2
    turned = jnp.concatenate([-values[..., half:], values[..., :half]], axis=-1)
    return values * cosine_table[..., None, :] + turned * sine_table[..., None, :]


def inverse_rotation(grads, cosine_table, sine_table):
    half = grads.shape[-1] // 2
    scaled = grads * sine_table[..., None, :]
    turned = jnp.concatenate([scaled[..., half:], -scaled[..., :half]], axis=-1)
    return grads * cosine_table[..., None, :] + turned


def norm_back(grad_hidden, normed, inverse, gain):
    scaled = grad_hidden * gain
    return inverse * (scaled - normed * jnp.mean(scaled * normed, axis=-1, keepdims=True))


def block_scores(
    query_rows_local, gathered_keys, block, span, query_pos, query_docs, all_docs, scale
):
    first_key = block * span
    key_rows = lax.dynamic_slice_in_dim(gathered_keys, first_key, span, 1)
    raw = (
        jnp.einsum(
            "sqcgd,skcd->scgqk", query_rows_local, key_rows, preferred_element_type=jnp.float32
        )
        * scale
    )
    key_pos = first_key + jnp.arange(span, dtype=jnp.int32)
    key_docs = lax.dynamic_slice_in_dim(all_docs, first_key, span, 1)
    allowed = (key_pos[None, None, :] <= query_pos[None, :, None]) & (
        key_docs[:, None, :] == query_docs[:, :, None]
    )
    return (jnp.where(allowed[:, None, None], raw, MASKED), key_rows)


def attend_forward(
    query_rows_local, gathered_keys, gathered_values, query_pos, query_docs, all_docs, count, span
):
    local_sequences, sequence_piece, heads_kv, query_group, width = query_rows_local.shape
    scale = 1.0 / math.sqrt(width)

    def step(block, carry):
        peak, total_count, accum = carry
        scores, unused = block_scores(
            query_rows_local, gathered_keys, block, span, query_pos, query_docs, all_docs, scale
        )
        new_peak = jnp.maximum(peak, jnp.max(scores, axis=-1))
        factor = jnp.exp(peak - new_peak)
        powers = jnp.exp(scores - new_peak[..., None])
        total_count = total_count * factor + jnp.sum(powers, axis=-1)
        value_rows = lax.dynamic_slice_in_dim(gathered_values, block * span, span, 1)
        accum = accum * jnp.transpose(factor, (0, 3, 1, 2))[..., None] + jnp.einsum(
            "scgqk,skcd->sqcgd",
            powers.astype(jnp.bfloat16),
            value_rows,
            preferred_element_type=jnp.float32,
        )
        return (new_peak, total_count, accum)

    start_peak = jnp.full(
        (local_sequences, heads_kv, query_group, sequence_piece), MASKED, jnp.float32
    )
    zero_out = jnp.zeros(
        (local_sequences, sequence_piece, heads_kv, query_group, width), jnp.float32
    )
    peak, total_count, accum = lax.fori_loop(
        0, count, step, (start_peak, jnp.zeros_like(start_peak), zero_out)
    )
    attended = accum / jnp.transpose(total_count, (0, 3, 1, 2))[..., None]
    return (attended, peak + jnp.log(total_count))


def attend_backward(
    query_rows_local,
    gathered_keys,
    gathered_values,
    heads_gradient,
    delta,
    log_sum,
    query_pos,
    query_docs,
    all_docs,
    count,
    span,
):
    local_sequences, sequence_piece, heads_kv, query_group, width = query_rows_local.shape
    sequence_length = gathered_keys.shape[1]
    scale = 1.0 / math.sqrt(width)

    def step(block, carry):
        grad_query, grad_keys, grad_values = carry
        scores, key_rows = block_scores(
            query_rows_local, gathered_keys, block, span, query_pos, query_docs, all_docs, scale
        )
        value_rows = lax.dynamic_slice_in_dim(gathered_values, block * span, span, 1)
        probs = jnp.exp(scores - log_sum[..., None])
        grad_probs = jnp.einsum(
            "sqcgd,skcd->scgqk", heads_gradient, value_rows, preferred_element_type=jnp.float32
        )
        grad_scores = (probs * (grad_probs - delta[..., None])).astype(jnp.bfloat16)
        grad_query = (
            grad_query
            + jnp.einsum(
                "scgqk,skcd->sqcgd", grad_scores, key_rows, preferred_element_type=jnp.float32
            )
            * scale
        )
        key_part = (
            jnp.einsum(
                "scgqk,sqcgd->skcd",
                grad_scores,
                query_rows_local,
                preferred_element_type=jnp.float32,
            )
            * scale
        )
        value_part = jnp.einsum(
            "scgqk,sqcgd->skcd",
            probs.astype(jnp.bfloat16),
            heads_gradient,
            preferred_element_type=jnp.float32,
        )
        grad_keys = lax.dynamic_update_slice_in_dim(
            grad_keys, key_part.reshape(local_sequences, span, heads_kv * width), block * span, 1
        )
        grad_values = lax.dynamic_update_slice_in_dim(
            grad_values,
            value_part.reshape(local_sequences, span, heads_kv * width),
            block * span,
            1,
        )
        return (grad_query, grad_keys, grad_values)

    start = (
        jnp.zeros((local_sequences, sequence_piece, heads_kv, query_group, width), jnp.float32),
        jnp.zeros((local_sequences, sequence_length, heads_kv * width), jnp.float32),
        jnp.zeros((local_sequences, sequence_length, heads_kv * width), jnp.float32),
    )
    return lax.fori_loop(0, count, step, start)


def body(
    tokens,
    doc_lengths,
    first_gain,
    query_weight,
    key_matrix,
    value_matrix,
    output_weight,
    second_gain,
    gate_weight,
    up_weight,
    down_weight,
    cotangent,
):
    micro_count, local_sequences, sequence_piece, width = tokens.shape
    query_group = QUERY_HEADS // KEY_VALUE_HEADS
    piece_index = lax.axis_index("seq")
    sequence_length = sequence_piece * lax.axis_size("seq")
    span = min(512, sequence_length)
    offset = piece_index * sequence_piece
    query_pos = offset + jnp.arange(sequence_piece, dtype=jnp.int32)
    count = (offset + sequence_piece + span - 1) // span
    shards = (
        query_weight,
        key_matrix,
        value_matrix,
        output_weight,
        gate_weight,
        up_weight,
        down_weight,
        first_gain,
        second_gain,
    )
    totals = [
        jnp.zeros((MODEL_WIDTH, QUERY_HEADS * HEAD_SIZE), jnp.float32),
        jnp.zeros((MODEL_WIDTH, KEY_VALUE_HEADS * HEAD_SIZE), jnp.float32),
        jnp.zeros((MODEL_WIDTH, KEY_VALUE_HEADS * HEAD_SIZE), jnp.float32),
        jnp.zeros((QUERY_HEADS * HEAD_SIZE, MODEL_WIDTH), jnp.float32),
        jnp.zeros((MODEL_WIDTH, FF), jnp.float32),
        jnp.zeros((MODEL_WIDTH, FF), jnp.float32),
        jnp.zeros((FF, MODEL_WIDTH), jnp.float32),
        jnp.zeros((MODEL_WIDTH,), jnp.float32),
        jnp.zeros((MODEL_WIDTH,), jnp.float32),
    ]
    outputs = []
    input_grads = []
    for micro_step in range(micro_count):
        gathered = fetch(shards)
        (
            full_query,
            full_key,
            full_value,
            full_output,
            full_gate,
            full_up,
            full_down,
            gain_one,
            gain_two,
        ) = gathered
        gain_one = gain_one.astype(jnp.float32)
        gain_two = gain_two.astype(jnp.float32)
        rows_in = tokens[micro_step].astype(jnp.float32)
        all_docs, all_pos = doc_tables(doc_lengths[micro_step], sequence_length)
        query_docs = lax.dynamic_slice_in_dim(all_docs, offset, sequence_piece, 1)
        cosine_table, sine_table = rope_tables(
            lax.dynamic_slice_in_dim(all_pos, offset, sequence_piece, 1), HEAD_SIZE
        )
        inverse_one = lax.rsqrt(jnp.mean(rows_in * rows_in, axis=-1, keepdims=True) + EPS)
        normed_one = rows_in * inverse_one
        hidden_one = (normed_one * gain_one).astype(jnp.bfloat16)
        query_projected = jnp.dot(hidden_one, full_query, preferred_element_type=jnp.float32)
        key_projected = jnp.dot(hidden_one, full_key, preferred_element_type=jnp.float32)
        value_projected = jnp.dot(hidden_one, full_value, preferred_element_type=jnp.float32)
        query_rows_local = apply_rotation(
            query_projected.reshape(local_sequences, sequence_piece, QUERY_HEADS, HEAD_SIZE),
            cosine_table,
            sine_table,
        ).astype(jnp.bfloat16)
        query_rows_local = query_rows_local.reshape(
            local_sequences, sequence_piece, KEY_VALUE_HEADS, query_group, HEAD_SIZE
        )
        local_keys = apply_rotation(
            key_projected.reshape(local_sequences, sequence_piece, KEY_VALUE_HEADS, HEAD_SIZE),
            cosine_table,
            sine_table,
        ).astype(jnp.bfloat16)
        local_keys = local_keys.reshape(
            local_sequences, sequence_piece, KEY_VALUE_HEADS * HEAD_SIZE
        )
        values_here = value_projected.astype(jnp.bfloat16)
        gathered_keys, gathered_values = (
            lax.all_gather(local_keys, "seq", axis=1, tiled=True),
            lax.all_gather(values_here, "seq", axis=1, tiled=True),
        )
        gathered_keys = gathered_keys.reshape(
            local_sequences, sequence_length, KEY_VALUE_HEADS, HEAD_SIZE
        )
        gathered_values = gathered_values.reshape(
            local_sequences, sequence_length, KEY_VALUE_HEADS, HEAD_SIZE
        )
        heads_out, log_sum = attend_forward(
            query_rows_local,
            gathered_keys,
            gathered_values,
            query_pos,
            query_docs,
            all_docs,
            count,
            span,
        )
        attended = heads_out.astype(jnp.bfloat16).reshape(
            local_sequences, sequence_piece, QUERY_HEADS * HEAD_SIZE
        )
        middle = rows_in + jnp.dot(attended, full_output, preferred_element_type=jnp.float32)
        inverse_two = lax.rsqrt(jnp.mean(middle * middle, axis=-1, keepdims=True) + EPS)
        normed_two = middle * inverse_two
        hidden_two = (normed_two * gain_two).astype(jnp.bfloat16)
        gate = jnp.dot(hidden_two, full_gate, preferred_element_type=jnp.float32)
        up_part = jnp.dot(hidden_two, full_up, preferred_element_type=jnp.float32)
        sigma = jax.nn.sigmoid(gate)
        product = (gate * sigma * up_part).astype(jnp.bfloat16)
        outputs.append(
            (middle + jnp.dot(product, full_down, preferred_element_type=jnp.float32)).astype(
                jnp.bfloat16
            )
        )
        grad_out = cotangent[micro_step]
        totals[6] = totals[6] + jnp.einsum(
            "scf,scd->fd", product, grad_out, preferred_element_type=jnp.float32
        )
        grad_product = jnp.einsum(
            "scd,fd->scf", grad_out, full_down, preferred_element_type=jnp.float32
        )
        grad_up = (grad_product * gate * sigma).astype(jnp.bfloat16)
        grad_gate = (grad_product * up_part * sigma * (1.0 + gate * (1.0 - sigma))).astype(
            jnp.bfloat16
        )
        totals[4] = totals[4] + jnp.einsum(
            "sce,scf->ef", hidden_two, grad_gate, preferred_element_type=jnp.float32
        )
        totals[5] = totals[5] + jnp.einsum(
            "sce,scf->ef", hidden_two, grad_up, preferred_element_type=jnp.float32
        )
        grad_hidden_two = jnp.einsum(
            "scf,ef->sce", grad_gate, full_gate, preferred_element_type=jnp.float32
        ) + jnp.einsum("scf,ef->sce", grad_up, full_up, preferred_element_type=jnp.float32)
        totals[8] = totals[8] + jnp.sum(grad_hidden_two * normed_two, axis=(0, 1))
        grad_middle = grad_out.astype(jnp.float32) + norm_back(
            grad_hidden_two, normed_two, inverse_two, gain_two
        )
        grad_branch = grad_middle.astype(jnp.bfloat16)
        totals[3] = totals[3] + jnp.einsum(
            "sce,scd->ed", attended, grad_branch, preferred_element_type=jnp.float32
        )
        heads_gradient = jnp.einsum(
            "scd,ed->sce", grad_branch, full_output, preferred_element_type=jnp.float32
        ).astype(jnp.bfloat16)
        heads_gradient = heads_gradient.reshape(
            local_sequences, sequence_piece, KEY_VALUE_HEADS, query_group, HEAD_SIZE
        )
        delta = jnp.einsum(
            "sqcgd,sqcgd->scgq",
            heads_gradient.astype(jnp.float32),
            heads_out,
            precision=lax.Precision.HIGHEST,
        )
        grad_query, grad_keys, grad_values = attend_backward(
            query_rows_local,
            gathered_keys,
            gathered_values,
            heads_gradient,
            delta,
            log_sum,
            query_pos,
            query_docs,
            all_docs,
            count,
            span,
        )
        returned_keys, values_back = (
            lax.psum_scatter(
                grad_keys.astype(jnp.bfloat16), "seq", scatter_dimension=1, tiled=True
            ).astype(jnp.float32),
            lax.psum_scatter(
                grad_values.astype(jnp.bfloat16), "seq", scatter_dimension=1, tiled=True
            ).astype(jnp.float32),
        )
        query_low = inverse_rotation(
            grad_query.reshape(local_sequences, sequence_piece, QUERY_HEADS, HEAD_SIZE),
            cosine_table,
            sine_table,
        ).astype(jnp.bfloat16)
        query_low = query_low.reshape(local_sequences, sequence_piece, QUERY_HEADS * HEAD_SIZE)
        key_reduced = inverse_rotation(
            returned_keys.reshape(local_sequences, sequence_piece, KEY_VALUE_HEADS, HEAD_SIZE),
            cosine_table,
            sine_table,
        ).astype(jnp.bfloat16)
        key_reduced = key_reduced.reshape(
            local_sequences, sequence_piece, KEY_VALUE_HEADS * HEAD_SIZE
        )
        value_low = values_back.astype(jnp.bfloat16)
        totals[0] = totals[0] + jnp.einsum(
            "sce,scf->ef", hidden_one, query_low, preferred_element_type=jnp.float32
        )
        totals[1] = totals[1] + jnp.einsum(
            "sce,scf->ef", hidden_one, key_reduced, preferred_element_type=jnp.float32
        )
        totals[2] = totals[2] + jnp.einsum(
            "sce,scf->ef", hidden_one, value_low, preferred_element_type=jnp.float32
        )
        grad_hidden_one = (
            jnp.einsum("scf,ef->sce", query_low, full_query, preferred_element_type=jnp.float32)
            + jnp.einsum("scf,ef->sce", key_reduced, full_key, preferred_element_type=jnp.float32)
            + jnp.einsum("scf,ef->sce", value_low, full_value, preferred_element_type=jnp.float32)
        )
        totals[7] = totals[7] + jnp.sum(grad_hidden_one * normed_one, axis=(0, 1))
        input_grads.append(
            (grad_middle + norm_back(grad_hidden_one, normed_one, inverse_one, gain_one)).astype(
                jnp.bfloat16
            )
        )
    seq_parts = (
        lax.psum_scatter(
            totals[0].astype(jnp.bfloat16), "seq", scatter_dimension=1, tiled=True
        ).astype(jnp.float32),
        lax.psum_scatter(
            totals[1].astype(jnp.bfloat16), "seq", scatter_dimension=1, tiled=True
        ).astype(jnp.float32),
        lax.psum_scatter(
            totals[2].astype(jnp.bfloat16), "seq", scatter_dimension=1, tiled=True
        ).astype(jnp.float32),
        lax.psum_scatter(
            totals[3].astype(jnp.bfloat16), "seq", scatter_dimension=1, tiled=True
        ).astype(jnp.float32),
        lax.psum_scatter(
            totals[4].astype(jnp.bfloat16), "seq", scatter_dimension=1, tiled=True
        ).astype(jnp.float32),
        lax.psum_scatter(
            totals[5].astype(jnp.bfloat16), "seq", scatter_dimension=1, tiled=True
        ).astype(jnp.float32),
        lax.psum_scatter(
            totals[6].astype(jnp.bfloat16), "seq", scatter_dimension=1, tiled=True
        ).astype(jnp.float32),
        lax.psum_scatter(
            totals[7].astype(jnp.bfloat16), "seq", scatter_dimension=0, tiled=True
        ).astype(jnp.float32),
        lax.psum_scatter(
            totals[8].astype(jnp.bfloat16), "seq", scatter_dimension=0, tiled=True
        ).astype(jnp.float32),
    )
    owned = (
        lax.psum_scatter(
            seq_parts[0].astype(jnp.bfloat16), "batch", scatter_dimension=0, tiled=True
        ).astype(jnp.float32),
        lax.psum_scatter(
            seq_parts[1].astype(jnp.bfloat16), "batch", scatter_dimension=0, tiled=True
        ).astype(jnp.float32),
        lax.psum_scatter(
            seq_parts[2].astype(jnp.bfloat16), "batch", scatter_dimension=0, tiled=True
        ).astype(jnp.float32),
        lax.psum_scatter(
            seq_parts[3].astype(jnp.bfloat16), "batch", scatter_dimension=0, tiled=True
        ).astype(jnp.float32),
        lax.psum_scatter(
            seq_parts[4].astype(jnp.bfloat16), "batch", scatter_dimension=0, tiled=True
        ).astype(jnp.float32),
        lax.psum_scatter(
            seq_parts[5].astype(jnp.bfloat16), "batch", scatter_dimension=0, tiled=True
        ).astype(jnp.float32),
        lax.psum_scatter(
            seq_parts[6].astype(jnp.bfloat16), "batch", scatter_dimension=0, tiled=True
        ).astype(jnp.float32),
    )
    gain_sums = lax.psum((seq_parts[7], seq_parts[8]), "batch")
    gain_first, gain_second = (gain_sums[0], gain_sums[1])
    return (
        jnp.stack(outputs),
        jnp.stack(input_grads),
        gain_first,
        owned[0],
        owned[1],
        owned[2],
        owned[3],
        gain_second,
        owned[4],
        owned[5],
        owned[6],
    )


def solution(mesh):
    return jax.shard_map(
        body,
        mesh=mesh,
        in_specs=(
            P(None, "batch", "seq", None),
            P(None, "batch", None),
            P("seq"),
            P("batch", "seq"),
            P("batch", "seq"),
            P("batch", "seq"),
            P("batch", "seq"),
            P("seq"),
            P("batch", "seq"),
            P("batch", "seq"),
            P("batch", "seq"),
            P(None, "batch", "seq", None),
        ),
        out_specs=(
            P(None, "batch", "seq", None),
            P(None, "batch", "seq", None),
            P("seq"),
            P("batch", "seq"),
            P("batch", "seq"),
            P("batch", "seq"),
            P("batch", "seq"),
            P("seq"),
            P("batch", "seq"),
            P("batch", "seq"),
            P("batch", "seq"),
        ),
        check_vma=False,
    )
```

profile of v0, /device:TPU:0, one launch (start us, length us, event | category | flops | bytes accessed | tf_op | source)
XLA Modules:
  0.0 1400.0 jit_solution(15732209100786617017)
XLA Ops:
  8.3 13.4 all-gather.4
  21.8 25.1 %all-gather.5 = bf16[32,6,576]{2,1,0:T(8,128)(2,1)S(1)} all-gather(bf16[1,6,576]{2,1,0:T(8,128)(2,1)S(1)} %bitcast.897), channel_id=1, replica_groups=mesh['batch'=4,'seq'=32] {'seq'}, dimensions={0}, use_global_device_ids=true | all-gather | bytes 228096 | tf_op jit(solution)/shard_map/all_gather | solution.py:32
  52.0 65.3 %all-reduce.12 = (bf16[576]{0:T(1024)(128)(2,1)S(1)}, bf16[576]{0:T(1024)(128)(2,1)S(1)}) all-reduce(bf16[576]{0:T(1024)(128)(2,1)S(1)} %dynamic-update-slice, bf16[576]{0:T(1024)(128)(2,1)S(1)} %dynamic-update-slice.1), channel_id=1, replica_groups=mesh['batch'=4,'seq'=32] {'seq'}, use_global_device_ids=true, to_apply=%add | all-reduce | flops 1152 | bytes 4608
  120.2 11.9 all-gather.8
  132.2 21.9 %all-gather.9 = bf16[32,6,576]{2,1,0:T(8,128)(2,1)S(1)} all-gather(bf16[1,6,576]{2,1,0:T(8,128)(2,1)S(1)} %bitcast.898), channel_id=1, replica_groups=mesh['batch'=4,'seq'=32] {'seq'}, dimensions={0}, use_global_device_ids=true | all-gather | bytes 228096 | tf_op jit(solution)/shard_map/all_gather | solution.py:33
  157.6 11.9 all-gather.12
  170.4 12.0 all-gather.13
  183.3 12.7 all_gather.92
  197.3 11.9 all-gather.6
  209.4 25.0 %all-gather.7 = bf16[32,18,576]{2,1,0:T(8,128)(2,1)S(1)} all-gather(bf16[1,18,576]{2,1,0:T(8,128)(2,1)S(1)} %bitcast.893), channel_id=1, replica_groups=mesh['batch'=4,'seq'=32] {'seq'}, dimensions={0}, use_global_device_ids=true | all-gather | bytes 684288 | tf_op jit(solution)/shard_map/all_gather | solution.py:31
  236.4 11.9 all-gather.10
  248.5 22.5 %all-gather.11 = bf16[32,18,576]{2,1,0:T(8,128)(2,1)S(1)} all-gather(bf16[1,18,576]{2,1,0:T(8,128)(2,1)S(1)} %bitcast.894), channel_id=1, replica_groups=mesh['batch'=4,'seq'=32] {'seq'}, dimensions={0}, use_global_device_ids=true | all-gather | bytes 684288 | tf_op jit(solution)/shard_map/all_gather | solution.py:34
  279.6 17.7 %all-gather.29.cloned.1.call-done = bf16[4096,192]{0,1:T(8,128)(2,1)} async-done(((bf16[128,192]{0,1:T(8,128)(2,1)}), bf16[4096,192]{0,1:T(8,128)(2,1)}) %all-gather.29.cloned.1.call-update) | async-done | bytes 1572880 | tf_op jit(solution)/shard_map/all_gather | solution.py:296
  304.9 37.6 %all-gather.23.cloned.1.call-done = bf16[576,1536]{0,1:T(8,128)(2,1)} async-done(((bf16[576,48]{0,1:T(8,128)(2,1)}), bf16[576,1536]{0,1:T(8,128)(2,1)}) %all-gather.23.cloned.1.call-update) | async-done | bytes 1769488 | tf_op jit(solution)/shard_map/all_gather | solution.py:35
  345.8 41.8 %all-gather.25.cloned.1.call-done = bf16[576,1536]{0,1:T(8,128)(2,1)} async-done(((bf16[576,48]{0,1:T(8,128)(2,1)}), bf16[576,1536]{0,1:T(8,128)(2,1)}) %all-gather.25.cloned.1.call-update) | async-done | bytes 1769488 | tf_op jit(solution)/shard_map/all_gather | solution.py:36
  390.8 42.4 %all-gather.35.cloned.1.call-done = bf16[32,18,1536]{2,1,0:T(8,128)(2,1)} async-done(((bf16[1,18,1536]{2,1,0:T(8,128)(2,1)}), bf16[32,18,1536]{2,1,0:T(8,128)(2,1)}) %all-gather.35.cloned.1.call-update) | async-done | bytes 1769488 | tf_op jit(solution)/shard_map/all_gather | solution.py:37
  450.4 78.9 %fusion.8 = bf16[1536,24]{0,1:T(8,128)(2,1)} fusion(bf16[1536,576]{0,1:T(8,128)(2,1)} %add_convert_fusion.2), kind=kCustom, calls=%all-reduce-scatter | all-reduce-scatter fusion | flops 1179649 | bytes 1843712
  558.6 12.6 concatenate.136
  575.8 15.8 %while.63 = (s32[]{:T(128)}, f32[1,128,3,3,64]{1,4,3,2,0:T(8,128)S(1)}, bf16[1,4096,192]{1,2,0:T(8,128)(2,1)}, bf16[1,4096,192]{1,2,0:T(8,128)(2,1)}, s32[]{:T(1...) while((s32[]{:T(128)}, ...), condition=%wide.region_26.27_spmd.clone, body=%wide.region_25.26_spmd.clone.sunk | while | flops 383926912 | bytes 13788407 | solution.py:201
  677.8 61.4 %reduce-scatter.46.cloned.1.call-done = bf16[128,192]{1,0:T(8,128)(2,1)} async-done(((bf16[4096,192]{1,0:T(8,128)(2,1)}), bf16[128,192]{1,0:T(8,128)(2,1)}) %reduce-scatter.46.cloned.1.call-update) | async-done | bytes 49168
  740.4 80.8 %reduce-scatter.48.cloned.1.call-done = bf16[128,192]{1,0:T(8,128)(2,1)} async-done(((bf16[4096,192]{1,0:T(8,128)(2,1)}), bf16[128,192]{1,0:T(8,128)(2,1)}) %reduce-scatter.48.cloned.1.call-update) | async-done | bytes 49168
  822.2 81.1 %reduce-scatter.42.cloned.1.call-done = bf16[128,192]{1,0:T(8,128)(2,1)} async-done(((bf16[4096,192]{1,0:T(8,128)(2,1)}), bf16[128,192]{1,0:T(8,128)(2,1)}) %reduce-scatter.42.cloned.1.call-update) | async-done | bytes 49168
  904.4 80.8 %reduce-scatter.44.cloned.1.call-done = bf16[128,192]{1,0:T(8,128)(2,1)} async-done(((bf16[4096,192]{1,0:T(8,128)(2,1)}), bf16[128,192]{1,0:T(8,128)(2,1)}) %reduce-scatter.44.cloned.1.call-update) | async-done | bytes 49168
  990.6 63.3 %all-reduce.11 = (bf16[576]{0:T(1024)(128)(2,1)S(1)}, bf16[576]{0:T(1024)(128)(2,1)S(1)}) all-reduce(bf16[576]{0:T(1024)(128)(2,1)S(1)} %add_convert_fusion.8, bf16[576]{0:T(1024)(128)(2,1)S(1)} %add_convert_fusion.7), channel_id=10, replica_groups=mesh['batch'=4,'seq'=32] {'seq'}, use_global_device_ids=true, to_apply=%region_32.33.clone | all-reduce | flops 1152 | bytes 4608
  1067.6 78.1 %reduce-scatter.40.cloned.1.call-done = bf16[576,48]{0,1:T(8,128)(2,1)} async-done(((bf16[576,1536]{0,1:T(8,128)(2,1)}), bf16[576,48]{0,1:T(8,128)(2,1)}) %reduce-scatter.40.cloned.1.call-update) | async-done | bytes 55312 | tf_op jit(solution)/shard_map/reduce_scatter | solution.py:442
  1147.4 108.4 %all-reduce.16.cloned.1.call-done = (bf16[576,576]{0,1:T(8,128)(2,1)}, bf16[576,192]{0,1:T(8,128)(2,1)}, bf16[576,192]{0,1:T(8,128)(2,1)}, bf16[576,576]{0,1:T(8,128)(2,1)}) async-done(((bf16[576,576]{0,1:T(8,128)(2,1)}, bf16[576,192]{0,1:T(8,128)(2,1)}, bf16[576,192]{0,1:T(8,128)(2,1)}, bf16[576,576]{0,1:T(8,128)(2,1)}), (bf16[576,576]{0,1:T(8,128)(2,1)}, bf16[576,192]{0,1:T(8,128)(2,1)}, ...) | async-done | bytes 1769488
  1262.4 11.2 all-reduce.10
  1279.8 21.0 %reduce-scatter.60.cloned.1.call-done = bf16[144,48]{1,0:T(8,128)(2,1)} async-done(((bf16[576,48]{1,0:T(8,128)(2,1)}), bf16[144,48]{1,0:T(8,128)(2,1)}) %reduce-scatter.60.cloned.1.call-update) | async-done | bytes 13840
  1302.3 21.2 %reduce-scatter.52.cloned.1.call-done = bf16[144,6]{1,0:T(8,128)(2,1)} async-done(((bf16[576,6]{1,0:T(8,128)(2,1)}), bf16[144,6]{1,0:T(8,128)(2,1)}) %reduce-scatter.52.cloned.1.call-update) | async-done | bytes 1744
  1325.0 21.2 %reduce-scatter.54.cloned.1.call-done = bf16[144,6]{1,0:T(8,128)(2,1)} async-done(((bf16[576,6]{1,0:T(8,128)(2,1)}), bf16[144,6]{1,0:T(8,128)(2,1)}) %reduce-scatter.54.cloned.1.call-update) | async-done | bytes 1744
  1347.6 21.2 %reduce-scatter.50.cloned.1.call-done = bf16[144,18]{1,0:T(8,128)(2,1)} async-done(((bf16[576,18]{1,0:T(8,128)(2,1)}), bf16[144,18]{1,0:T(8,128)(2,1)}) %reduce-scatter.50.cloned.1.call-update) | async-done | bytes 5200
  1370.3 21.2 %reduce-scatter.56.cloned.1.call-done = bf16[144,18]{1,0:T(8,128)(2,1)} async-done(((bf16[576,18]{1,0:T(8,128)(2,1)}), bf16[144,18]{1,0:T(8,128)(2,1)}) %reduce-scatter.56.cloned.1.call-update) | async-done | bytes 5200
  (461 shorter events, 242.4 us)
Async XLA Ops:
  7.2 267.0 %all-gather.31.cloned.1.call-start = ((), (), s32[]{:S(2)}) async-start(), calls=%async_computation.19 | async-start | bytes 1622016 | tf_op jit(solution)/shard_map/all_gather | solution.py:295
  8.3 187.8 %copy-start.55 = (s32[4096]{0:T(1024)}, s32[4096]{0:T(1024)S(1)}, u32[]{:S(2)}) copy-start(s32[4096]{0:T(1024)S(1)} %fusion.188) | copy-start | bytes 49156
  48.2 186.6 %copy-start.70 = (f32[128]{0:T(128)}, f32[128]{0:T(128)S(1)}, u32[]{:S(2)}) copy-start(f32[128]{0:T(128)S(1)} %add_rsqrt_fusion.1) | copy-start | bytes 1540
  120.1 154.1 %all-gather.33.cloned.1.call-start = ((), (), s32[]{:S(2)}) async-start(), calls=%async_computation.20 | async-start | bytes 1622016 | tf_op jit(solution)/shard_map/all_gather | solution.py:296
  155.3 124.3 %all-gather.27.cloned.1.call-start = ((), (), s32[]{:S(2)}) async-start(), calls=%async_computation.17 | async-start | bytes 1622016 | tf_op jit(solution)/shard_map/all_gather | solution.py:295
  156.5 140.8 %all-gather.29.cloned.1.call-start = ((), (), s32[]{:S(2)}) async-start(), calls=%async_computation.18 | async-start | bytes 1622016 | tf_op jit(solution)/shard_map/all_gather | solution.py:296
  157.5 185.0 %all-gather.23.cloned.1.call-start = ((), (), s32[]{:S(2)}) async-start(), calls=%async_computation.13 | async-start | bytes 2027520 | tf_op jit(solution)/shard_map/all_gather | solution.py:35
  170.4 217.2 %all-gather.25.cloned.1.call-start = ((), (), s32[]{:S(2)}) async-start(), calls=%async_computation.14 | async-start | bytes 2027520 | tf_op jit(solution)/shard_map/all_gather | solution.py:36
  183.3 250.0 %all-gather.35.cloned.1.call-start = ((), (), s32[]{:S(2)}) async-start(), calls=%async_computation.21 | async-start | bytes 2433024 | tf_op jit(solution)/shard_map/all_gather | solution.py:37
  196.0 480.2 %reduce-scatter.62.cloned.1.call-start = ((), (), s32[]{:S(2)}) async-start(), calls=%async_computation.32 | async-start | bytes 491520
  530.4 17.4 %collective-permute-start.6 = (bf16[1536,24]{0,1:T(8,128)(2,1)}, bf16[1536,24]{0,1:T(8,128)(2,1)S(1)}, u32[]{:S(2)}, u32[]{:S(2)}) collective-permute-start(bf16[1536,24]{0,1:T(8,128)(2,1)} %fusion.8), channel_id=1, source_target_pairs={{0,7},{1,8},{2,9},{3,10},{4,11},{5,12},{6,13},{7,14},{8,15},{9,16}... | collective-permute-start | bytes 221192
  531.7 21.6 %collective-permute-start.5 = (bf16[1536,24]{0,1:T(8,128)(2,1)}, bf16[1536,24]{0,1:T(8,128)(2,1)S(1)}, u32[]{:S(2)}, u32[]{:S(2)}) collective-permute-start(bf16[1536,24]{0,1:T(8,128)(2,1)} %fusion.8), channel_id=1, source_target_pairs={{0,6},{1,7},{2,8},{3,9},{4,10},{5,11},{6,12},{7,13},{8,14},{9,15},... | collective-permute-start | bytes 221192
  533.0 24.7 %collective-permute-start.4 = (bf16[1536,24]{0,1:T(8,128)(2,1)}, bf16[1536,24]{0,1:T(8,128)(2,1)S(1)}, u32[]{:S(2)}, u32[]{:S(2)}) collective-permute-start(bf16[1536,24]{0,1:T(8,128)(2,1)} %fusion.8), channel_id=1, source_target_pairs={{0,5},{1,6},{2,7},{3,8},{4,9},{5,10},{6,11},{7,12},{8,13},{9,14},{... | collective-permute-start | bytes 221192
  534.3 23.5 %collective-permute-start.3 = (bf16[1536,24]{0,1:T(8,128)(2,1)}, bf16[1536,24]{0,1:T(8,128)(2,1)S(1)}, u32[]{:S(2)}, u32[]{:S(2)}) collective-permute-start(bf16[1536,24]{0,1:T(8,128)(2,1)} %fusion.8), channel_id=1, source_target_pairs={{0,4},{1,5},{2,6},{3,7},{4,8},{5,9},{6,10},{7,11},{8,12},{9,13},{1... | collective-permute-start | bytes 221192
  539.8 6.7 collective-permute-start.7
  546.5 11.3 collective-permute-start.2
  547.8 10.0 collective-permute-start.1
  553.3 5.3 collective-permute-start
  573.1 166.1 %reduce-scatter.46.cloned.1.call-start = ((), (), s32[]{:S(2)}) async-start(), calls=%async_computation.24 | async-start | bytes 2162688
  605.4 215.8 %reduce-scatter.48.cloned.1.call-start = ((), (), s32[]{:S(2)}) async-start(), calls=%async_computation.25 | async-start | bytes 2162688
  620.4 282.8 %reduce-scatter.42.cloned.1.call-start = ((), (), s32[]{:S(2)}) async-start(), calls=%async_computation.22 | async-start | bytes 2162688
  644.4 340.8 %reduce-scatter.44.cloned.1.call-start = ((), (), s32[]{:S(2)}) async-start(), calls=%async_computation.23 | async-start | bytes 2162688
  659.7 406.1 %reduce-scatter.38.cloned.1.call-start = ((), (), s32[]{:S(2)}) async-start(), calls=%async_computation.15 | async-start | bytes 2027520 | tf_op jit(solution)/shard_map/reduce_scatter | solution.py:439
  667.1 478.6 %reduce-scatter.40.cloned.1.call-start = ((), (), s32[]{:S(2)}) async-start(), calls=%async_computation.16 | async-start | bytes 2027520 | tf_op jit(solution)/shard_map/reduce_scatter | solution.py:442
  676.1 579.6 %all-reduce.16.cloned.1.call-start = ((), (), s32[]{:S(2)}) async-start(), calls=%async_computation.33 | async-start | bytes 3932160
  740.3 246.7 %copy-start.22 = (bf16[192,576]{1,0:T(8,128)(2,1)S(1)}, bf16[192,576]{1,0:T(8,128)(2,1)}, u32[]{:S(2)}) copy-start(bf16[192,576]{1,0:T(8,128)(2,1)} %copy-done.21) | copy-start | bytes 663556
  990.6 287.7 %reduce-scatter.58.cloned.1.call-start = ((), (), s32[]{:S(2)}) async-start(), calls=%async_computation.30 | async-start | bytes 184320
  1067.4 233.4 %reduce-scatter.60.cloned.1.call-start = ((), (), s32[]{:S(2)}) async-start(), calls=%async_computation.31 | async-start | bytes 184320
  1147.3 176.2 %reduce-scatter.52.cloned.1.call-start = ((), (), s32[]{:S(2)}) async-start(), calls=%async_computation.27 | async-start | bytes 184320
  1257.3 88.9 %reduce-scatter.54.cloned.1.call-start = ((), (), s32[]{:S(2)}) async-start(), calls=%async_computation.28 | async-start | bytes 184320
  1258.9 109.9 %reduce-scatter.50.cloned.1.call-start = ((), (), s32[]{:S(2)}) async-start(), calls=%async_computation.26 | async-start | bytes 184320
  1260.6 130.9 %reduce-scatter.56.cloned.1.call-start = ((), (), s32[]{:S(2)}) async-start(), calls=%async_computation.29 | async-start | bytes 184320
  (81 other events, 1621.3 us)
Sparse Core Ops, SparseCore 0:
  120.3 39.8 all-gather.30
  162.9 43.1 all-gather.32
  208.9 43.1 all-gather.26
  254.2 43.1 all-gather.28
  299.5 42.9 all-gather.22
  344.7 42.8 all-gather.24
  389.8 43.3 all-gather.34
  573.2 24.0 reduce-scatter.61
  605.5 133.6 reduce-scatter.45
  743.0 78.1 reduce-scatter.47
  825.1 78.1 reduce-scatter.41
  907.1 78.1 reduce-scatter.43
  989.3 76.4 reduce-scatter.37
  1069.2 76.4 reduce-scatter.39
  1149.6 106.0 all-reduce.15
  1258.1 20.2 reduce-scatter.57
  1280.5 20.2 reduce-scatter.59
  1303.2 20.2 reduce-scatter.51
  1325.8 20.2 reduce-scatter.53
  1348.5 20.2 reduce-scatter.49
  1371.2 20.2 reduce-scatter.55
where the time goes:
time: 1410 us; the launch traced here: 1400 us
  waiting for transfers between devices  753 us (53%)
  blocking collectives  399 us (28%)
  local copies, waits for them, and re-layouts  116 us (8%)
  matrix products  62.4 us (4%)
  starting transfers between devices  22.1 us (2%)
  other arithmetic  20 us (1%)
  between operations  19 us (1%)
    unnamed x41, waiting for transfers between devices  525 us
    unnamed x3, blocking collectives  207 us
    unnamed x221, local copies, waits for them, and re-layouts  105 us
    reduce_scatter x1, waiting for transfers between devices, body(): lax.psum_scatter(totals[5].astype(jnp.bfloat16), 'seq', scatter_dimension...  78.1 us
    all_gather x1, waiting for transfers between devices, fetch(): lax.all_gather(tall[6], 'seq', axis=1, tiled=True)  42.4 us
    all_gather x1, waiting for transfers between devices, fetch(): lax.all_gather(tall[5], 'seq', axis=1, tiled=True)  41.8 us
    all_gather x1, waiting for transfers between devices, fetch(): lax.all_gather(tall[4], 'seq', axis=1, tiled=True)  37.6 us
  transfers between devices with their start and end apart: 29, of which 19 were waited for; matrix products, arithmetic and copies ran while one was open for 11% of the time, Pallas kernels for 0%

commit v1 on v0

v1 whole, which is shorter than its diff:
```python
import numpy as np
import ml_dtypes
import jax
import jax.numpy as jnp
from jax import lax
from jax.experimental import pallas as pl
from jax.experimental.pallas import tpu as pltpu
from jax.sharding import PartitionSpec as P

D = 576
HEADS = 9
KV = 3
HD = 64
FF = 1536
PIECE = 128
T = 2 * PIECE
LANES = 3 * T
EPS = 1e-05
THETA = 100000.0
MASKED = -1e30
MESH = pl.DeviceIdType.MESH
F32 = jnp.float32
BF16 = jnp.bfloat16
VLIMIT = 58 * 1024 * 1024


def spread_matrix():
    m = np.zeros((960, 1024), np.float32)
    n = np.arange(576)
    m[n, 32 * (n // 18) + n % 18] = 1
    n = np.arange(192)
    m[576 + n, 32 * (n // 6) + 18 + n % 6] = 1
    m[768 + n, 32 * (n // 6) + 24 + n % 6] = 1
    return m.astype(ml_dtypes.bfloat16)


def gain_matrix():
    n = np.arange(576)
    fold = np.zeros((576, 576), np.float32)
    for b in range(4):
        fold[n, 144 * b + n % 18] = 1
    owner = (n[None, :] // 18 == np.arange(32)[:, None]).astype(np.float32)
    return fold.astype(ml_dtypes.bfloat16), owner


def nn(a, b):
    return lax.dot_general(a, b, (((1,), (0,)), ((), ())), preferred_element_type=F32)


def nt(a, b):
    return lax.dot_general(a, b, (((1,), (1,)), ((), ())), preferred_element_type=F32)


def tn(a, b):
    return lax.dot_general(a, b, (((0,), (0,)), ((), ())), preferred_element_type=F32)


def rcopy(src, dst, ss, rs, dev):
    return pltpu.make_async_remote_copy(
        src_ref=src, dst_ref=dst, send_sem=ss, recv_sem=rs, device_id=dev, device_id_type=MESH
    )


def place():
    b = lax.axis_index("batch")
    s = lax.axis_index("seq")
    c = lax.rem(s, 2)
    p = lax.div(s, 2)
    return b, s, c, p, lax.div(p, 4), lax.rem(p, 4)


def seq_of(y, x, c):
    return (y * 4 + x) * 2 + c


def hop(i, d):
    return lax.rem(i + d, 4)


def hail(devices):
    bar = pltpu.get_barrier_semaphore()
    for dev in devices:
        pl.semaphore_signal(bar, inc=1, device_id=dev, device_id_type=MESH)
    return bar


def grid_partners(b, s, c, y, x):
    found = [(b, seq_of(y, x, 1 - c))]
    for d in (1, 2, 3):
        found += [
            (hop(b, d), s),
            (b, seq_of(y, hop(x, d), c)),
            (b, seq_of(hop(y, d), x, c)),
        ]
    return found


W_ORDER = (0, 3, 1, 2)


class Ring:
    def __init__(self, dev, ss, rs):
        self.dev, self.ss, self.rs = dev, ss, rs

    def copy(self, n, src, dst):
        du, dv = {0: (1, 0), 1: (3, 0), 2: (1, 0), 3: (3, 0)}.get(n, (0, 1 if n // 4 in (1, 3) else 3))
        return rcopy(src, dst, self.ss.at[n], self.rs.at[n], self.dev(du, dv))


def gather_kernel(
    wq, wk, wv, wo, wg, wu, wd, gains, tokens, cot, tok_o, cot_o, g_o,
    raw_f, dwn_f, raw, dwn, za, zd, blk, zsem, lsem, rsem, cs, zz, zl,
):
    b, s, c, p, y, x = place()
    early = jnp.minimum(s, 31 - s)
    slot = lax.div(s, 16)
    bar = hail(grid_partners(b, s, c, y, x))
    for src in (p, 31 - p):
        @pl.when(src != s)
        def _():
            pl.semaphore_signal(bar, inc=1, device_id=(b, src), device_id_type=MESH)
    raw_f[...] = jnp.zeros_like(raw_f)
    dwn_f[...] = jnp.zeros_like(dwn_f)
    for at, ref in ((0, wq), (18, wk), (24, wv), (32, wo), (64, wg), (112, wu)):
        raw_f[at : at + ref.shape[0], :] = ref[...].astype(F32)
    raw_f[30:32, 0:18] = gains[...].astype(F32)
    dwn_f[0:18, :] = wd[...].astype(F32)
    raw[...] = raw_f[...].astype(BF16)
    dwn[...] = dwn_f[...].astype(BF16)
    own_target = jnp.where(2 * early == s, 1, 0) + jnp.where(2 * early + 1 == s, 1, 0)
    pl.semaphore_wait(bar, 12 - own_target)

    za[pl.ds(b, 1)] = raw[...][None]
    zd[pl.ds(b, 1)] = dwn[...][None]

    def zcopies(n, at, part):
        dev = (hop(b, 1 if n in (0, 2) else 3), s)
        found = []
        for k, (ref, rows) in enumerate(((za, 80), (zd, 16))):
            view = ref.at[at] if part is None else ref.at[at, pl.ds(rows * part, rows)]
            found.append(rcopy(view, view, zsem.at[0, k, n], zsem.at[1, k, n], dev))
        return found

    def start(copies):
        for cp in copies:
            cp.start()

    zsent = [zcopies(0, b, None), zcopies(1, b, None)]
    start(zsent[0] + zsent[1])

    for m in (0, 1):
        dst = 2 * early + m
        for k, (src_ref, dst_ref) in enumerate(((tokens, tok_o), (cot, cot_o))):
            @pl.when(dst != s)
            def _():
                rcopy(src_ref.at[m], dst_ref.at[slot], zz.at[0, k, m], zz.at[1, k, slot], (b, dst)).start()

            @pl.when(dst == s)
            def _():
                pltpu.make_async_copy(src_ref.at[m], dst_ref.at[slot], zl.at[k]).start()

    for n, way in ((0, 3), (1, 1)):
        for cp in zcopies(n, hop(b, way), None):
            cp.wait_recv()
        zsent.append(zcopies(2 + n, hop(b, way), n))
        start(zsent[-1])
    for n in (2, 3):
        for cp in zcopies(n, hop(b, 2), n - 2):
            cp.wait_recv()
    main = jnp.concatenate([za[i].astype(F32) for i in range(4)], axis=1).astype(BF16)
    down = jnp.concatenate([zd[i] for i in range(4)], axis=1)
    blk[0:160, :] = main
    blk[160:256, 512:576] = jnp.zeros((96, 64), BF16)
    for k in range(3):
        blk[160 + 32 * k : 192 + 32 * k, 0:512] = down[:, 512 * k : 512 * (k + 1)]

    lc = pltpu.make_async_copy(blk, g_o.at[y, x, c], lsem)
    lc.start()
    other = (b, seq_of(y, x, 1 - c))
    sent = []
    swaps = []
    rings = []
    for h in (0, 1):
        def spot(du, dv):
            return (hop(y, dv), hop(x, du)) if h == 0 else (hop(y, du), hop(x, dv))

        def dev(du, dv, spot=spot):
            return (b, seq_of(*spot(du, dv), c))

        def view(du, dv, part=None, spot=spot, h=h):
            rows = pl.ds(128 * h, 128) if part is None else pl.ds(128 * h + 64 * part, 64)
            return g_o.at[(*spot(du, dv), c, rows)]

        rings.append((Ring(dev, rsem.at[0, h], rsem.at[1, h]), view))

    def go(h, n, src, dst):
        cp = rings[h][0].copy(n, src, dst)
        cp.start()
        sent.append(cp)

    def swap(h, du, dv, src=None):
        ref = rings[h][1](du, dv)
        n = 4 * dv + du
        cp = rcopy(ref if src is None else src, ref, cs.at[0, h, n], cs.at[1, h, n], other)
        cp.start()
        swaps.append(cp)

    def arrive(h, n, du, dv, part=None):
        ref = rings[h][1](du, dv, part)
        rings[h][0].copy(n, ref, ref).wait_recv()

    def pass_on(h, n, du, dv, part=None):
        ref = rings[h][1](du, dv, part)
        go(h, n, ref, ref)

    for h in (0, 1):
        src = blk.at[pl.ds(128 * h, 128)]
        dst = rings[h][1](0, 0)
        for n in (0, 1, 4, 8):
            go(h, n, src, dst)
        swap(h, 0, 0, src)
    for h in (0, 1):
        for n, du in ((0, 3), (1, 1)):
            arrive(h, n, du, 0)
            pass_on(h, 2 + n, du, 0, n)
            pass_on(h, 4 + du, du, 0)
            pass_on(h, 8 + du, du, 0)
            swap(h, du, 0)

    def line(h, w):
        arrive(h, 4 + w, w, 3)
        pass_on(h, 12 + w, w, 3, 0)
        swap(h, w, 3)
        arrive(h, 8 + w, w, 1)
        pass_on(h, 16 + w, w, 1, 1)
        swap(h, w, 1)

    for h in (0, 1):
        line(h, 0)
    for h in (0, 1):
        arrive(h, 2, 2, 0, 0)
        arrive(h, 3, 2, 0, 1)
        pass_on(h, 6, 2, 0)
        pass_on(h, 10, 2, 0)
        swap(h, 2, 0)
    for w in (3, 1, 2):
        for h in (0, 1):
            line(h, w)
    for w in W_ORDER:
        for h in (0, 1):
            arrive(h, 12 + w, w, 2, 0)
            arrive(h, 16 + w, w, 2, 1)
            swap(h, w, 2)
    lc.wait()
    for cp in sent:
        cp.wait_send()
    for cp in swaps:
        cp.wait()
    for group in zsent:
        for cp in group:
            cp.wait_send()

    for m in (0, 1):
        dst = 2 * early + m
        for k, (src_ref, dst_ref) in enumerate(((tokens, tok_o), (cot, cot_o))):
            @pl.when(dst != s)
            def _():
                rcopy(src_ref.at[m], dst_ref.at[slot], zz.at[0, k, m], zz.at[1, k, slot], (b, dst)).wait_send()

            @pl.when(dst == s)
            def _():
                pltpu.make_async_copy(src_ref.at[m], dst_ref.at[slot], zl.at[k]).wait()
    for q, src in enumerate((p, 31 - p)):
        for k, (src_ref, dst_ref) in enumerate(((tokens, tok_o), (cot, cot_o))):
            @pl.when(src != s)
            def _():
                rcopy(src_ref.at[0], dst_ref.at[q], zz.at[0, k, 0], zz.at[1, k, q], (b, src)).wait_recv()


def gather_call(shards, tokens, cot):
    dma = pltpu.SemaphoreType.DMA
    any_ = pl.BlockSpec(memory_space=pl.ANY)
    vm = pl.BlockSpec(memory_space=pltpu.VMEM)
    return pl.pallas_call(
        gather_kernel,
        out_shape=(
            jax.ShapeDtypeStruct((2, D, PIECE), BF16),
            jax.ShapeDtypeStruct((2, D, PIECE), BF16),
            jax.ShapeDtypeStruct((4, 4, 2, 256, D), BF16),
        ),
        in_specs=[vm] * 8 + [any_, any_],
        out_specs=(any_, any_, any_),
        scratch_shapes=[
            pltpu.VMEM((160, 144), F32),
            pltpu.VMEM((32, 384), F32),
            pltpu.VMEM((160, 144), BF16),
            pltpu.VMEM((32, 384), BF16),
            pltpu.VMEM((4, 160, 144), BF16),
            pltpu.VMEM((4, 32, 384), BF16),
            pltpu.VMEM((256, D), BF16),
            dma((2, 2, 4)),
            dma(()),
            dma((2, 2, 20)),
            dma((2, 2, 16)),
            dma((2, 2, 2)),
            dma((2,)),
        ],
        compiler_params=pltpu.CompilerParams(
            collective_id=0, has_side_effects=True, vmem_limit_bytes=VLIMIT
        ),
        name="gather_weights",
    )(*shards, tokens, cot)


def token_rows(ref):
    return jnp.concatenate([ref[0].astype(F32).T, ref[1].astype(F32).T], axis=0)


def gain_row(rows, fold, owner):
    spread = nt(rows, fold[:, 0:128])
    return jnp.sum(spread * owner, axis=0, keepdims=True)


def pre_kernel(g, tok, cos, sin, spread, fold, owner, kv_o, qt_o, h1_o):
    wa = g[:, :, :]
    g1 = gain_row(wa[:, 30, 0:128], fold[...], owner[...])
    w = nn(spread[...], wa.reshape(1024, D)).astype(BF16)
    x = token_rows(tok)
    r1 = lax.rsqrt(jnp.sum(x * x, axis=-1, keepdims=True) * (1.0 / D) + EPS)
    h1 = (x * r1 * g1).astype(BF16)
    h1_o[...] = h1
    z = nt(w, h1)
    co, si = cos[...], sin[...]

    def rot(u):
        u1, u2 = u[0:32], u[32:64]
        return jnp.concatenate([u1 * co - u2 * si, u2 * co + u1 * si], axis=0)

    for h in range(HEADS):
        q = (rot(z[64 * h : 64 * h + 64]).astype(BF16).astype(F32) * 0.125).astype(BF16)
        kvh, gi = h // 3, h % 3
        for piece in range(2):
            lane = piece * 384 + gi * 128
            qt_o[kvh, 0:64, lane : lane + 128] = q[:, piece * 128 : piece * 128 + 128]
    for h in range(KV):
        qt_o[h, 64:128, :] = jnp.zeros((64, LANES), BF16)
        k = rot(z[576 + 64 * h : 640 + 64 * h])
        v = z[768 + 64 * h : 832 + 64 * h]
        kv_o[h] = jnp.concatenate([k, v], axis=0).T.astype(BF16)


def with_row(blocks, row, values):
    at = lax.broadcasted_iota(jnp.int32, (1, 32, 1), 1)
    return jnp.where(at == row, values[:, None, :], blocks)


def whole(shape):
    return pl.BlockSpec(shape, lambda i: (0,) * len(shape))


def pre_call(g, tok, cos, sin, spread, fold, owner):
    vm = pl.BlockSpec(memory_space=pltpu.VMEM)
    return pl.pallas_call(
        pre_kernel,
        out_shape=(
            jax.ShapeDtypeStruct((KV, T, 128), BF16),
            jax.ShapeDtypeStruct((KV, 128, LANES), BF16),
            jax.ShapeDtypeStruct((T, D), BF16),
        ),
        grid=(1,),
        in_specs=[whole((32, 32, D))] + [vm] * 6,
        out_specs=(vm, vm, vm),
        compiler_params=pltpu.CompilerParams(vmem_limit_bytes=VLIMIT),
        name="project_qkv",
    )(g, tok, cos, sin, spread, fold, owner)


def diagonal_mask(p, qpos, qstart):
    row = lax.broadcasted_iota(jnp.int32, (T, 1), 0)
    kpos = jnp.where(row < PIECE, p * PIECE + row, (31 - p) * PIECE + row - PIECE)
    return (kpos <= qpos) & (kpos >= qstart)


def first_mask(qstart):
    row = lax.broadcasted_iota(jnp.int32, (PIECE, 1), 0)
    return row >= qstart


def plane_ring(b, c, p, y, x, ss, rs):
    u, v = jnp.where(c == 0, x, y), jnp.where(c == 0, y, x)
    su, sv = 1 + 3 * c, 4 - 3 * c

    def index(du, dv):
        return lax.rem(u + du, 4) * su + lax.rem(v + dv, 4) * sv

    def dev(du, dv):
        return (b, 2 * index(du, dv) + c)

    bar = pltpu.get_barrier_semaphore()
    for du, dv in ((1, 0), (3, 0), (0, 1), (0, 3)):
        pl.semaphore_signal(bar, inc=1, device_id=dev(du, dv), device_id_type=MESH)
    pl.semaphore_wait(bar, 4)
    return Ring(dev, ss, rs), index


def pick(i, values):
    found = values[0]
    for k, value in enumerate(values[1:]):
        found = jnp.where(i == k + 1, value, found)
    return found


FORWARD = ((0, 0), (3, 0), (1, 0), (0, 3), (0, 1), (2, 0), (3, 3), (3, 1), (1, 3), (1, 1), (2, 3), (2, 1), (0, 2), (3, 2), (1, 2), (2, 2))
BACKWARD = ((0, 0), (2, 2), (1, 2), (3, 2), (0, 2), (2, 1), (2, 3), (1, 1), (1, 3), (3, 1), (3, 3), (0, 1), (0, 3), (2, 0), (1, 0), (3, 0))
HALVES = (pl.ds(0, PIECE), pl.ds(PIECE, PIECE))


def attend_kernel(kv, qt, qpos, qstart, kv_o, att_o, lse_o, m_s, l_s, acc, ss, rs):
    b, s, c, p, y, x = place()
    ring, index = plane_ring(b, c, p, y, x, ss, rs)

    def view(du, dv, part=None):
        at = index(du, dv)
        return kv_o.at[at] if part is None else kv_o.at[at, :, HALVES[part]]

    def send(n, du, dv, part=None):
        ref = view(du, dv, part)
        return ring.copy(n, kv if (du, dv) == (0, 0) else ref, ref)

    def arrive(n, du, dv, part=None):
        ref = view(du, dv, part)
        ring.copy(n, ref, ref).wait_recv()

    own = [send(n, 0, 0) for n in (0, 1, 4, 8)]
    for cp in own:
        cp.start()

    def near(n, du):
        def event():
            arrive(n, du, 0)
            send(2 + n, du, 0, n).start()
            send(4 + du, du, 0).start()
            send(8 + du, du, 0).start()
        return event

    def far():
        arrive(2, 2, 0, 0)
        arrive(3, 2, 0, 1)
        send(6, 2, 0).start()
        send(10, 2, 0).start()

    def line(w):
        def event():
            arrive(4 + w, w, 3)
            send(12 + w, w, 3, 0).start()
            arrive(8 + w, w, 1)
            send(16 + w, w, 1, 1).start()
        return event

    def last(w):
        def event():
            arrive(12 + w, w, 2, 0)
            arrive(16 + w, w, 2, 1)
        return event

    events = {
        1: [near(0, 3), near(1, 1)], 2: [line(0)], 3: [far], 4: [line(3)], 5: [line(1)], 7: [line(2)],
        12: [last(0)], 13: [last(3)], 14: [last(1)], 15: [last(2)],
    }
    later = [(2, 3, 0, 0), (3, 1, 0, 1), (6, 2, 0, None), (10, 2, 0, None)]
    for du in (3, 1):
        later += [(4 + du, du, 0, None), (8 + du, du, 0, None)]
    for w in range(4):
        later += [(12 + w, w, 3, 0), (16 + w, w, 1, 1)]

    kv_o[pl.ds(p, 1)] = kv[...][None]
    m_s[...] = jnp.full_like(m_s, MASKED)
    l_s[...] = jnp.zeros_like(l_s)
    acc[...] = jnp.zeros_like(acc)

    def step(block, h, lanes, mask, drop):
        st = nn(block, qt[h, :, lanes])
        if mask is not None:
            st = jnp.where(mask, st, MASKED)
        m_old = m_s[h, :, lanes]
        top = jnp.max(st, axis=0, keepdims=True)
        if drop is None:
            m_new = jnp.maximum(m_old, top)
            m_sub = m_new
        else:
            m_new = jnp.maximum(m_old, jnp.where(drop, MASKED, top))
            m_sub = jnp.where(drop, -MASKED, m_new)
        pt = jnp.exp(st - m_sub)
        a = jnp.exp(m_old - m_new)
        m_s[h, :, lanes] = m_new
        l_s[h, :, lanes] = l_s[h, :, lanes] * a + jnp.sum(pt, axis=0, keepdims=True)
        acc[h, :, lanes] = acc[h, :, lanes] * a + tn(block, pt.astype(BF16))[64:128]

    every = pl.ds(0, LANES)
    late = pl.ds(384, 384)
    mask = diagonal_mask(p, qpos[...], qstart[...])
    for h in range(KV):
        step(kv[h], h, every, mask, None)

    def visit(i, carry):
        for k, todo in events.items():
            @pl.when(i == k)
            def _():
                for event in todo:
                    event()

        j = index(pick(i, [o[0] for o in FORWARD]), pick(i, [o[1] for o in FORWARD]))

        @pl.when((j < p) & (j > 0))
        def _():
            for h in range(KV):
                step(kv_o[j, h, 0:PIECE, :], h, every, None, None)

        @pl.when((j < p) & (j == 0))
        def _():
            keep = first_mask(qstart[...])
            for h in range(KV):
                step(kv_o[0, h, 0:PIECE, :], h, every, keep, None)

        @pl.when(j > p)
        def _():
            drop = qstart[:, late] >= PIECE
            for h in range(KV):
                step(kv_o[j, h], h, late, None, drop)

        return carry

    lax.fori_loop(1, 16, visit, 0)
    for h in range(KV):
        total = l_s[h]
        att_o[h] = acc[h] / total
        lse_o[h] = m_s[h] + jnp.log(total)

    for cp in own:
        cp.wait_send()
    for item in later:
        send(*item).wait_send()


def attend_call(kv, qt, qpos, qstart):
    vm = pl.BlockSpec(memory_space=pltpu.VMEM)
    dma = pltpu.SemaphoreType.DMA
    return pl.pallas_call(
        attend_kernel,
        out_shape=(
            jax.ShapeDtypeStruct((16, KV, T, 128), BF16),
            jax.ShapeDtypeStruct((KV, HD, LANES), F32),
            jax.ShapeDtypeStruct((KV, 1, LANES), F32),
        ),
        in_specs=[vm] * 4,
        out_specs=(vm, vm, vm),
        scratch_shapes=[
            pltpu.VMEM((KV, 1, LANES), F32),
            pltpu.VMEM((KV, 1, LANES), F32),
            pltpu.VMEM((KV, HD, LANES), F32),
            dma((20,)),
            dma((20,)),
        ],
        compiler_params=pltpu.CompilerParams(
            collective_id=1, has_side_effects=True, vmem_limit_bytes=VLIMIT
        ),
        name="attend_forward",
    )(kv, qt, qpos, qstart)


def mlp_kernel(
    g, tok, cot, att, spread, sprt, fold, owner,
    mixed_o, dmid_o, dot_o, delta_o, dw_o, wd, act_s, wo_s, h2_s, dh2_s, mix_s,
):
    p2 = spread[0:576, :]
    p2t = sprt[:, 0:576]
    owner_rows = owner[...]
    g2 = gain_row(g[:, 31, 0:128], fold[...], owner_rows)
    wo_s[...] = nn(p2, g[:, 32:64, :].reshape(1024, D)).astype(BF16)
    for k in range(3):
        third = g[:, 160 + 32 * k : 192 + 32 * k, 0:512].reshape(1024, 512)
        wd[:, 512 * k : 512 * k + 512] = nn(p2, third).astype(BF16)
    rows = []
    for h in range(HEADS):
        kvh, gi = h // 3, h % 3
        rows.append(
            jnp.concatenate(
                [att[kvh, :, q * 384 + gi * 128 : q * 384 + gi * 128 + 128] for q in range(2)], axis=1
            )
        )
    att_f = jnp.concatenate(rows, axis=0)
    att_t = att_f.T.astype(BF16)
    middle = token_rows(tok) + nt(att_t, wo_s[...])
    r2 = lax.rsqrt(jnp.sum(middle * middle, axis=-1, keepdims=True) * (1.0 / D) + EPS)
    n2 = middle * r2
    h2_s[...] = (n2 * g2).astype(BF16)
    mix_s[...] = middle
    dh2_s[...] = jnp.zeros_like(dh2_s)
    dy = token_rows(cot).astype(BF16)
    dyt_rows = jnp.concatenate([cot[0], cot[1]], axis=1)

    def chunk(f, carry):
        at = pl.ds(8 * f, 8)
        lanes = pl.ds(pl.multiple_of(384 * f, 128), 384)
        wg = g[at, 64:112, :].reshape(384, D)
        wu = g[at, 112:160, :].reshape(384, D)
        h2 = h2_s[...]
        gate = nt(h2, wg)
        up = nt(h2, wu)
        sig = 1.0 / (1.0 + jnp.exp(-gate))
        silu = gate * sig
        act = (silu * up).astype(BF16)
        act_s[:, lanes] = act
        wdf = wd[:, lanes]
        mix_s[...] += nt(act, wdf)
        da = nn(dy, wdf)
        dup = (da * silu).astype(BF16)
        dgate = (da * up * sig * (1.0 + gate * (1.0 - sig))).astype(BF16)
        dh2_s[...] += nn(dgate, wg) + nn(dup, wu)
        dw_o[at, 64:112, :] = tn(dgate, h2).astype(BF16).reshape(8, 48, D)
        dw_o[at, 112:160, :] = tn(dup, h2).astype(BF16).reshape(8, 48, D)
        return carry

    lax.fori_loop(0, 4, chunk, 0)
    for q in range(2):
        mixed_o[q] = mix_s[PIECE * q : PIECE * (q + 1), :].T.astype(BF16)
    dyt = nn(p2t, dyt_rows).astype(BF16)
    dw_o[:, 160:256, 512:576] = jnp.zeros((32, 96, 64), BF16)
    for k in range(3):
        part = nn(dyt, act_s[:, 512 * k : 512 * k + 512]).astype(BF16)
        dw_o[:, 160 + 32 * k : 192 + 32 * k, 0:512] = part.reshape(32, 32, 512)
    dh2 = dh2_s[...]
    gsum = jnp.sum(dh2 * n2, axis=0, keepdims=True)
    gain = nn((gsum * owner_rows).astype(BF16), fold[...])
    g2v = dh2 * g2
    dmid = dy.astype(F32) + r2 * (g2v - n2 * (jnp.sum(g2v * n2, axis=-1, keepdims=True) * (1.0 / D)))
    dmid_o[...] = dmid
    dbr = dmid.astype(BF16)
    dbt = nn(p2t, dmid.T.astype(BF16)).astype(BF16)
    dw_o[:, 32:64, :] = with_row(nn(dbt, att_t).reshape(32, 32, D), 18, gain).astype(BF16)
    dw_o[:, 0:32, :] = jnp.zeros((32, 32, D), BF16)
    datt = nn(dbr, wo_s[...]).astype(BF16).astype(F32).T
    for h in range(HEADS):
        kvh, gi = h // 3, h % 3
        for q in range(2):
            lane = q * 384 + gi * 128
            part = datt[64 * h : 64 * h + 64, 128 * q : 128 * q + 128]
            dot_o[kvh, 64:128, lane : lane + 128] = part.astype(BF16)
            delta_o[kvh, :, lane : lane + 128] = jnp.sum(
                part * att[kvh, :, lane : lane + 128], axis=0, keepdims=True
            )
    for h in range(KV):
        dot_o[h, 0:64, :] = jnp.zeros((64, LANES), BF16)


def mlp_call(g, tok, cot, att, spread, sprt, fold, owner):
    vm = pl.BlockSpec(memory_space=pltpu.VMEM)
    return pl.pallas_call(
        mlp_kernel,
        out_shape=(
            jax.ShapeDtypeStruct((2, D, PIECE), BF16),
            jax.ShapeDtypeStruct((T, D), F32),
            jax.ShapeDtypeStruct((KV, 128, LANES), BF16),
            jax.ShapeDtypeStruct((KV, 1, LANES), F32),
            jax.ShapeDtypeStruct((32, 256, D), BF16),
        ),
        in_specs=[vm] * 8,
        out_specs=(vm,) * 5,
        scratch_shapes=[
            pltpu.VMEM((D, FF), BF16),
            pltpu.VMEM((T, FF), BF16),
            pltpu.VMEM((D, D), BF16),
            pltpu.VMEM((T, D), BF16),
            pltpu.VMEM((T, D), F32),
            pltpu.VMEM((T, D), F32),
        ],
        compiler_params=pltpu.CompilerParams(vmem_limit_bytes=VLIMIT),
        name="feed_forward",
    )(g, tok, cot, att, spread, sprt, fold, owner)


def attend_back_kernel(
    kv, qt, dot, lse, delta, qpos, qstart, dq_o, dkv_o, sent, va, vb, vp, vm, ua, ub, up, um, ss, rs
):
    b, s, c, p, y, x = place()
    ring, index = plane_ring(b, c, p, y, x, ss, rs)
    lo, hi = HALVES
    dq_o[...] = jnp.zeros_like(dq_o)

    def view(du, dv, part=None):
        at = index(du, dv)
        return sent.at[at] if part is None else sent.at[at, :, HALVES[part]]

    def add(du, dv, buf, part=None):
        at = index(du, dv)
        for h in range(KV):
            if part is None:
                sent[at, h] = (sent[at, h].astype(F32) + buf[h].astype(F32)).astype(BF16)
            else:
                rows = slice(PIECE * part, PIECE * (part + 1))
                sent[at, h, rows, :] = (sent[at, h, rows, :].astype(F32) + buf[h].astype(F32)).astype(BF16)

    def link(n, src, dst):
        return ring.copy(n, src, dst)

    pieces = {}
    for w in range(4):
        pieces[12 + w] = (w, 2, 0, va.at[w])
        pieces[16 + w] = (w, 2, 1, vb.at[w])
        pieces[4 + w] = (w, 1, None, vp.at[w])
        pieces[8 + w] = (w, 3, None, vm.at[w])
    pieces[2] = (2, 0, 0, ua)
    pieces[3] = (2, 0, 1, ub)
    pieces[0] = (1, 0, None, up)
    pieces[1] = (3, 0, None, um)

    def send(n):
        du, dv, part, dst = pieces[n]
        return link(n, view(du, dv, part), dst)

    def event(du, dv):
        if dv == 2:
            send(12 + du).start()
            send(16 + du).start()
        elif dv == 1:
            send(12 + du).wait_recv()
            add(du, 1, va.at[du], 0)
            send(4 + du).start()
        elif dv == 3:
            send(16 + du).wait_recv()
            add(du, 3, vb.at[du], 1)
            send(8 + du).start()
        else:
            send(4 + du).wait_recv()
            send(8 + du).wait_recv()
            if du:
                add(du, 0, vp.at[du])
                add(du, 0, vm.at[du])
            if du == 2:
                send(2).start()
                send(3).start()
            elif du == 1:
                send(2).wait_recv()
                add(1, 0, ua, 0)
                send(0).start()
            elif du == 3:
                send(3).wait_recv()
                add(3, 0, ub, 1)
                send(1).start()

    def step(block, h, lanes, mask, drop):
        q = qt[h, :, lanes]
        do = dot[h, :, lanes]
        st = nn(block, q)
        if mask is not None:
            st = jnp.where(mask, st, MASKED)
        base = lse[h, :, lanes]
        if drop is not None:
            base = jnp.where(drop, -MASKED, base)
        pt = jnp.exp(st - base)
        dp = nn(block, do)
        ds = (pt * (dp - delta[h, :, lanes])).astype(BF16)
        dq_o[h, :, lanes] += tn(block, ds)[0:64]
        return nt(ds, q) + nt(pt.astype(BF16), do)

    every = pl.ds(0, LANES)
    late = pl.ds(384, 384)

    def visit(i, carry):
        j = index(pick(i, [o[0] for o in BACKWARD]), pick(i, [o[1] for o in BACKWARD]))

        @pl.when(j < p)
        def _():
            sent[j, :, PIECE:T, :] = jnp.zeros((KV, PIECE, 128), BF16)

        @pl.when((j < p) & (j > 0))
        def _():
            for h in range(KV):
                sent[j, h, 0:PIECE, :] = step(kv[j, h, 0:PIECE, :], h, every, None, None).astype(BF16)

        @pl.when((j < p) & (j == 0))
        def _():
            keep = first_mask(qstart[...])
            for h in range(KV):
                sent[0, h, 0:PIECE, :] = step(kv[0, h, 0:PIECE, :], h, every, keep, None).astype(BF16)

        @pl.when(j > p)
        def _():
            drop = qstart[:, late] >= PIECE
            for h in range(KV):
                sent[j, h] = step(kv[j, h], h, late, None, drop).astype(BF16)

        for k, offset in enumerate(BACKWARD):
            if k:
                @pl.when(i == k)
                def _():
                    event(*offset)

        return carry

    lax.fori_loop(1, 16, visit, 0)
    mask = diagonal_mask(p, qpos[...], qstart[...])
    for h in range(KV):
        dkv_o[h] = step(kv[p, h], h, every, mask, None)

    event(0, 0)
    send(0).wait_recv()
    send(1).wait_recv()
    for h in range(KV):
        total = dkv_o[h] + vp[0, h].astype(F32) + vm[0, h].astype(F32)
        dkv_o[h] = total + up[h].astype(F32) + um[h].astype(F32)
    for n in pieces:
        send(n).wait_send()


def attend_back_call(kv, qt, dot, lse, delta, qpos, qstart):
    vm = pl.BlockSpec(memory_space=pltpu.VMEM)
    dma = pltpu.SemaphoreType.DMA
    return pl.pallas_call(
        attend_back_kernel,
        out_shape=(
            jax.ShapeDtypeStruct((KV, HD, LANES), F32),
            jax.ShapeDtypeStruct((KV, T, 128), F32),
        ),
        in_specs=[vm] * 7,
        out_specs=(vm, vm),
        scratch_shapes=[
            pltpu.VMEM((16, KV, T, 128), BF16),
            pltpu.VMEM((4, KV, PIECE, 128), BF16),
            pltpu.VMEM((4, KV, PIECE, 128), BF16),
            pltpu.VMEM((4, KV, T, 128), BF16),
            pltpu.VMEM((4, KV, T, 128), BF16),
            pltpu.VMEM((KV, PIECE, 128), BF16),
            pltpu.VMEM((KV, PIECE, 128), BF16),
            pltpu.VMEM((KV, T, 128), BF16),
            pltpu.VMEM((KV, T, 128), BF16),
            dma((20,)),
            dma((20,)),
        ],
        compiler_params=pltpu.CompilerParams(
            collective_id=2, has_side_effects=True, vmem_limit_bytes=VLIMIT
        ),
        name="attend_backward",
    )(kv, qt, dot, lse, delta, qpos, qstart)


def post_kernel(
    dw_in, g, tok, h1, dq, dkv, dmid, cos, sin, sprt, fold, owner, tg_o, dw_o, stage, sem
):
    co, si = cos[...], sin[...]

    def unrot(u):
        u1, u2 = u[0:32], u[32:64]
        return jnp.concatenate([u1 * co + u2 * si, u2 * co - u1 * si], axis=0)

    rows, vals = [], []
    for h in range(HEADS):
        kvh, gi = h // 3, h % 3
        part = jnp.concatenate(
            [dq[kvh, :, q * 384 + gi * 128 : q * 384 + gi * 128 + 128] for q in range(2)], axis=1
        )
        rows.append(unrot(part * 0.125))
    for h in range(KV):
        both = dkv[h].T
        rows.append(unrot(both[0:64]))
        vals.append(both[64:128])
    dz = jnp.concatenate(rows + vals, axis=0).astype(BF16)
    dzp = nn(sprt[...], dz).astype(BF16)
    wa = g[:, :, :]
    owner_rows = owner[...]
    g1 = gain_row(wa[:, 30, 0:128], fold[...], owner_rows)
    dh1 = tn(dzp, wa.reshape(1024, D))
    x = token_rows(tok)
    r1 = lax.rsqrt(jnp.sum(x * x, axis=-1, keepdims=True) * (1.0 / D) + EPS)
    n1 = x * r1
    gsum = jnp.sum(dh1 * n1, axis=0, keepdims=True)
    gain = nn((gsum * owner_rows).astype(BF16), fold[...])
    stage[...] = with_row(nn(dzp, h1[...]).reshape(32, 32, D), 30, gain).astype(BF16)
    g1v = dh1 * g1
    tg = dmid[...] + r1 * (g1v - n1 * (jnp.sum(g1v * n1, axis=-1, keepdims=True) * (1.0 / D)))
    for q in range(2):
        tg_o[q] = tg[PIECE * q : PIECE * (q + 1), :].T.astype(BF16)
    cp = pltpu.make_async_copy(stage, dw_o.at[:, 0:32], sem)
    cp.start()
    cp.wait()


def post_call(dw, g, tok, h1, dq, dkv, dmid, cos, sin, sprt, fold, owner):
    vm = pl.BlockSpec(memory_space=pltpu.VMEM)
    any_ = pl.BlockSpec(memory_space=pl.ANY)
    return pl.pallas_call(
        post_kernel,
        out_shape=(
            jax.ShapeDtypeStruct((2, D, PIECE), BF16),
            jax.ShapeDtypeStruct((32, 256, D), BF16),
        ),
        grid=(1,),
        in_specs=[any_, whole((32, 32, D))] + [vm] * 10,
        out_specs=(vm, any_),
        scratch_shapes=[pltpu.VMEM((32, 32, D), BF16), pltpu.SemaphoreType.DMA(())],
        input_output_aliases={0: 1},
        compiler_params=pltpu.CompilerParams(vmem_limit_bytes=VLIMIT),
        name="project_back",
    )(dw, g, tok, h1, dq, dkv, dmid, cos, sin, sprt, fold, owner)


def scatter_kernel(
    dw, mixed, tgrad, mixed_o, tgrad_o, raw_o, down_o,
    own, r0, va, vb, vp, vm, ua, ub, up, um, zs, zd, za, zb, zp, zm, ya, yb, yp, ym,
    c0, lsem, rsem, zsem, zz, zl,
):
    b, s, c, p, y, x = place()
    early = jnp.minimum(s, 31 - s)
    slot = lax.div(s, 16)
    bar = hail(grid_partners(b, s, c, y, x))
    for m in (0, 1):
        src = 2 * early + m
        @pl.when(src != s)
        def _():
            pl.semaphore_signal(bar, inc=1, device_id=(b, src), device_id_type=MESH)
    own_target = jnp.where(2 * early == s, 1, 0) + jnp.where(2 * early + 1 == s, 1, 0)
    pl.semaphore_wait(bar, 12 - own_target)
    other = (b, seq_of(y, x, 1 - c))

    order = [(dy, dx) for dy in range(4) for dx in range(4)]
    far = [o for o in order if 2 in o]
    mid = [o for o in order if 2 not in o and 0 not in o]
    near = [o for o in order if 2 not in o and 0 in o]
    near.sort(key=lambda o: o == (0, 0))
    fold = {}
    for o in far + mid + near:
        dy, dx = o
        n = 4 * dy + dx
        yy, xx = hop(y, dy), hop(x, dx)
        cp = rcopy(dw.at[yy, xx, 1 - c], r0.at[yy, xx], c0.at[0, n], c0.at[1, n], other)
        lc = pltpu.make_async_copy(dw.at[yy, xx, c], own.at[yy, xx], lsem.at[n])
        cp.start()
        lc.start()
        fold[o] = (cp, lc)

    for q, dst in enumerate((p, 31 - p)):
        for k, (src_ref, dst_ref) in enumerate(((mixed, mixed_o), (tgrad, tgrad_o))):
            @pl.when(dst != s)
            def _():
                rcopy(src_ref.at[q], dst_ref.at[c], zz.at[0, k, q], zz.at[1, k, c], (b, dst)).start()

            @pl.when(dst == s)
            def _():
                pltpu.make_async_copy(src_ref.at[q], dst_ref.at[c], zl.at[k]).start()

    sent = []
    rings = []
    for h in (0, 1):
        def spot(du, dv, h=h):
            return (hop(y, dv), hop(x, du)) if h == 0 else (hop(y, du), hop(x, dv))

        def dev(du, dv, spot=spot):
            return (b, seq_of(*spot(du, dv), c))

        rings.append((Ring(dev, rsem.at[0, h], rsem.at[1, h]), spot))

    def rows(h, part=None):
        return pl.ds(128 * h, 128) if part is None else pl.ds(128 * h + 64 * part, 64)

    landing = []
    for h in (0, 1):
        found = {}
        for w in range(4):
            found[12 + w] = (w, 2, 0, va.at[h, w])
            found[16 + w] = (w, 2, 1, vb.at[h, w])
            found[4 + w] = (w, 1, None, vp.at[h, w])
            found[8 + w] = (w, 3, None, vm.at[h, w])
        found[2] = (2, 0, 0, ua.at[h])
        found[3] = (2, 0, 1, ub.at[h])
        found[0] = (1, 0, None, up.at[h])
        found[1] = (3, 0, None, um.at[h])
        landing.append(found)

    def link(h, n):
        du, dv, part, dst = landing[h][n]
        ring, spot = rings[h]
        return ring.copy(n, own.at[(*spot(du, dv), rows(h, part))], dst)

    def go(h, *numbers):
        for n in numbers:
            cp = link(h, n)
            cp.start()
            sent.append(cp)

    def add(h, du, dv, part, *refs):
        at = (*rings[h][1](du, dv), rows(h, part))
        total = own[at].astype(F32)
        for ref in refs:
            total += ref[...].astype(F32)
        own[at] = total.astype(BF16)

    def folded(offsets):
        for o in offsets:
            cp, lc = fold[o]
            lc.wait()
            cp.wait_recv()
            at = (hop(y, o[0]), hop(x, o[1]))
            own[at] = (own[at].astype(F32) + r0[at].astype(F32)).astype(BF16)

    def sides(h, w):
        link(h, 12 + w).wait_recv()
        add(h, w, 1, 0, va.at[h, w])
        go(h, 4 + w)
        link(h, 16 + w).wait_recv()
        add(h, w, 3, 1, vb.at[h, w])
        go(h, 8 + w)

    def home(h, w):
        link(h, 4 + w).wait_recv()
        link(h, 8 + w).wait_recv()
        add(h, w, 0, None, vp.at[h, w], vm.at[h, w])
        if w == 2:
            go(h, 2, 3)
        elif w == 1:
            link(h, 2).wait_recv()
            add(h, 1, 0, 0, ua.at[h])
            go(h, 0)
        elif w == 3:
            link(h, 3).wait_recv()
            add(h, 3, 0, 1, ub.at[h])
            go(h, 1)

    folded(far)
    for w in (2, 1, 3, 0):
        for h in (0, 1):
            go(h, 12 + w, 16 + w)
    folded(mid)
    for w in (2, 1, 3):
        for h in (0, 1):
            sides(h, w)
    folded(near)
    for h in (0, 1):
        sides(h, 0)
    for w in (2, 1, 3, 0):
        for h in (0, 1):
            home(h, w)
    final = []
    for h in (0, 1):
        link(h, 0).wait_recv()
        link(h, 1).wait_recv()
        final.append(own[y, x, rows(h)].astype(F32) + up[h].astype(F32) + um[h].astype(F32))
    fa, fb = final
    main = jnp.concatenate([fa, fb[0:32]], axis=0)
    down = jnp.concatenate([fb[32 + 32 * k : 64 + 32 * k, 0:512] for k in range(3)], axis=1)
    for k in range(4):
        zs[k] = main[:, 144 * k : 144 * k + 144].astype(BF16)
        zd[k] = down[:, 384 * k : 384 * k + 384].astype(BF16)

    def zlink(n):
        at = hop(b, 2 if n > 1 else 1 + 2 * n)
        dev = (hop(b, 1 if n in (0, 2) else 3), s)
        found = []
        for k, (ref, size, dst) in enumerate(((zs, 80, (zp, zm, za, zb)[n]), (zd, 16, (yp, ym, ya, yb)[n]))):
            src = ref.at[at] if n < 2 else ref.at[at, pl.ds(size * (n - 2), size)]
            found.append(rcopy(src, dst, zsem.at[0, k, n], zsem.at[1, k, n], dev))
        return found

    def zgo(n):
        for cp in zlink(n):
            cp.start()
            sent.append(cp)

    def zarrive(n):
        for cp in zlink(n):
            cp.wait_recv()

    zgo(2)
    zgo(3)
    for n, bufs in ((2, (za, ya)), (3, (zb, yb))):
        zarrive(n)
        at = hop(b, 1 if n == 2 else 3)
        for ref, size, buf in ((zs, 80, bufs[0]), (zd, 16, bufs[1])):
            part = (at, pl.ds(size * (n - 2), size))
            ref[part] = (ref[part].astype(F32) + buf[...].astype(F32)).astype(BF16)
        zgo(n - 2)
    zarrive(0)
    zarrive(1)
    raw_o[...] = zs[b].astype(F32) + zp[...].astype(F32) + zm[...].astype(F32)
    down_o[...] = zd[b].astype(F32) + yp[...].astype(F32) + ym[...].astype(F32)
    for cp, lc in fold.values():
        cp.wait_send()
    for cp in sent:
        cp.wait_send()
    for q, dst in enumerate((p, 31 - p)):
        for k, (src_ref, dst_ref) in enumerate(((mixed, mixed_o), (tgrad, tgrad_o))):
            @pl.when(dst != s)
            def _():
                rcopy(src_ref.at[q], dst_ref.at[c], zz.at[0, k, q], zz.at[1, k, c], (b, dst)).wait_send()

            @pl.when(dst == s)
            def _():
                pltpu.make_async_copy(src_ref.at[q], dst_ref.at[c], zl.at[k]).wait()
    for m in (0, 1):
        src = 2 * early + m
        for k, (src_ref, dst_ref) in enumerate(((mixed, mixed_o), (tgrad, tgrad_o))):
            @pl.when(src != s)
            def _():
                rcopy(src_ref.at[0], dst_ref.at[m], zz.at[0, k, 0], zz.at[1, k, m], (b, src)).wait_recv()


def scatter_call(dw, mixed, tgrad):
    dma = pltpu.SemaphoreType.DMA
    any_ = pl.BlockSpec(memory_space=pl.ANY)
    vm = pl.BlockSpec(memory_space=pltpu.VMEM)
    return pl.pallas_call(
        scatter_kernel,
        out_shape=(
            jax.ShapeDtypeStruct((2, D, PIECE), BF16),
            jax.ShapeDtypeStruct((2, D, PIECE), BF16),
            jax.ShapeDtypeStruct((160, 144), F32),
            jax.ShapeDtypeStruct((32, 384), F32),
        ),
        in_specs=[any_, any_, any_],
        out_specs=(any_, any_, vm, vm),
        scratch_shapes=[
            pltpu.VMEM((4, 4, 256, D), BF16),
            pltpu.VMEM((4, 4, 256, D), BF16),
            pltpu.VMEM((2, 4, 64, D), BF16),
            pltpu.VMEM((2, 4, 64, D), BF16),
            pltpu.VMEM((2, 4, 128, D), BF16),
            pltpu.VMEM((2, 4, 128, D), BF16),
            pltpu.VMEM((2, 64, D), BF16),
            pltpu.VMEM((2, 64, D), BF16),
            pltpu.VMEM((2, 128, D), BF16),
            pltpu.VMEM((2, 128, D), BF16),
            pltpu.VMEM((4, 160, 144), BF16),
            pltpu.VMEM((4, 32, 384), BF16),
            pltpu.VMEM((80, 144), BF16),
            pltpu.VMEM((80, 144), BF16),
            pltpu.VMEM((160, 144), BF16),
            pltpu.VMEM((160, 144), BF16),
            pltpu.VMEM((16, 384), BF16),
            pltpu.VMEM((16, 384), BF16),
            pltpu.VMEM((32, 384), BF16),
            pltpu.VMEM((32, 384), BF16),
            dma((2, 16)),
            dma((16,)),
            dma((2, 2, 20)),
            dma((2, 2, 4)),
            dma((2, 2, 2)),
            dma((2,)),
        ],
        compiler_params=pltpu.CompilerParams(
            collective_id=3, has_side_effects=True, vmem_limit_bytes=VLIMIT
        ),
        name="scatter_grads",
    )(dw, mixed, tgrad)


def finish_kernel(mixed, tgrad, raw, down, mixed_o, tgrad_o, g1, wq, wk, wv, wo, g2, wg, wu, wd):
    mixed_o[...] = mixed[...]
    tgrad_o[...] = tgrad[...]
    g1[...] = raw[30:31, 0:18]
    g2[...] = raw[50:51, 0:18]
    for at, ref in ((0, wq), (18, wk), (24, wv), (32, wo), (64, wg), (112, wu)):
        ref[...] = raw[at : at + ref.shape[0], :]
    wd[...] = down[0:18, :]


def finish_call(mixed, tgrad, raw, down):
    vm = pl.BlockSpec(memory_space=pltpu.VMEM)
    shapes = [(1, 18), (18, 144), (6, 144), (6, 144), (18, 144), (1, 18), (48, 144), (48, 144), (18, 384)]
    return pl.pallas_call(
        finish_kernel,
        out_shape=tuple([jax.ShapeDtypeStruct((2, D, PIECE), BF16)] * 2 + [jax.ShapeDtypeStruct(n, F32) for n in shapes]),
        in_specs=[vm] * 4,
        out_specs=(vm,) * 11,
        name="write_outputs",
    )(mixed, tgrad, raw, down)


def body(
    tokens, doc_lengths, first_gain, query_weight, key_matrix, value_matrix,
    output_weight, second_gain, gate_weight, up_weight, down_weight, cotangent,
):
    s = lax.axis_index("seq")
    c, p = s % 2, s // 2
    gains = jnp.stack([first_gain, second_gain])
    spread = jnp.asarray(spread_matrix())
    sprt = jnp.asarray(spread_matrix().T.copy())
    fold, owner = (jnp.asarray(m) for m in gain_matrix())

    lens = lax.dynamic_index_in_dim(doc_lengths[:, 0, :], c, 0, False)
    starts = [jnp.zeros((), jnp.int32), lens[0], lens[0] + lens[1]]
    at = jnp.arange(PIECE, dtype=jnp.int32)
    spots = jnp.stack([p * PIECE + at, (31 - p) * PIECE + at])
    begins = jnp.where(spots >= starts[2], starts[2], jnp.where(spots >= starts[1], starts[1], 0))
    rates = THETA ** (-2.0 * jnp.arange(HD // 2, dtype=F32) / HD)
    angles = (spots - begins).reshape(T).astype(F32)[None, :] * rates[:, None]
    cos, sin = jnp.cos(angles), jnp.sin(angles)
    qpos = jnp.broadcast_to(spots[:, None], (2, 3, PIECE)).reshape(1, LANES)
    qstart = jnp.broadcast_to(begins[:, None], (2, 3, PIECE)).reshape(1, LANES)

    shards = [
        query_weight.T, key_matrix.T, value_matrix.T, output_weight.T,
        gate_weight.T, up_weight.T, down_weight.T, gains,
    ]
    turn = lambda a: jnp.swapaxes(a[:, 0], 1, 2)
    tok, cot, gathered = gather_call(shards, turn(tokens), turn(cotangent))
    g = gathered.reshape(32, 256, D)
    kv, qt, h1 = pre_call(g, tok, cos, sin, spread, fold, owner)
    kv_all, att, lse = attend_call(kv, qt, qpos, qstart)
    mixed, dmid, dot, delta, dw = mlp_call(g, tok, cot, att, spread, sprt, fold, owner)
    dq, dkv = attend_back_call(kv_all, qt, dot, lse, delta, qpos, qstart)
    tgrad, dw = post_call(dw, g, tok, h1, dq, dkv, dmid, cos, sin, sprt, fold, owner)
    mixed, tgrad, raw, down = scatter_call(dw.reshape(4, 4, 2, 256, D), mixed, tgrad)
    mixed, tgrad, g1, wq, wk, wv, wo, g2, wg, wu, wd = finish_call(mixed, tgrad, raw, down)
    back = lambda a: jnp.swapaxes(a, 1, 2)[:, None]
    return (
        back(mixed), back(tgrad), g1.reshape(18), wq.T, wk.T, wv.T, wo.T, g2.reshape(18), wg.T, wu.T, wd.T,
    )


def solution(mesh):
    weight = P("batch", "seq")
    rows = P(None, "batch", "seq", None)
    return jax.shard_map(
        body,
        mesh=mesh,
        in_specs=(
            rows, P(None, "batch", None), P("seq"), weight, weight, weight, weight,
            P("seq"), weight, weight, weight, rows,
        ),
        out_specs=(
            rows, rows, P("seq"), weight, weight, weight, weight,
            P("seq"), weight, weight, weight,
        ),
        check_vma=False,
    )
```

time: 1410 us -> 221 us (0.16)
  waiting for transfers between devices: 753 us -> 0 us
  blocking collectives: 399 us -> 0 us
  Pallas kernels: 0 us -> 212 us
  local copies, waits for them, and re-layouts: 116 us -> 2.43 us
  matrix products: 62.4 us -> 0 us
  starting transfers between devices: 22.1 us -> 0 us
  between operations: 19 us -> 2.19 us
  other arithmetic: 20 us -> 3.34 us
    unnamed x41 -> x0, waiting for transfers between devices: 525 us -> none
    pallas_call x0 -> x8, Pallas kernels: none -> 212 us  [the longest x1 57.1 us: scatter_call(): pl.pallas_call(scatter_kernel, out_shape=(jax.ShapeDtypeStruct((2, D, PIE...]
    unnamed x3 -> x0, blocking collectives: 207 us -> none
    all_gather x11 -> x0, blocking collectives: 180 us -> none  [the longest x1 25.1 us: fetch(): lax.all_gather(tall[1], 'seq', axis=1, tiled=True)]
    all_gather x7 -> x0, waiting for transfers between devices: 140 us -> none  [the longest x1 42.4 us: fetch(): lax.all_gather(tall[6], 'seq', axis=1, tiled=True)]
    unnamed x221 -> x2, local copies, waits for them, and re-layouts: 105 us -> 0.65 us
    reduce_scatter x2 -> x0, waiting for transfers between devices: 89.1 us -> none  [the longest x1 78.1 us: body(): lax.psum_scatter(totals[5].astype(jnp.bfloat16), 'seq', scatter_dimension...]
    dot_general x56 -> x0, matrix products: 62.4 us -> none  [the longest x4 5.84 us: block_scores(): jnp.einsum('sqcgd,skcd->scgqk', query_rows_local, key_rows, preferred_ele...]
  transfers between devices with their start and end apart: 29 -> 0, of which waited for: 19 -> 0; matrix products, arithmetic and copies ran while one was open for 11% -> 0% of each run, Pallas kernels for 0% -> 0%
where the time goes in v1:
time: 221 us; the launch traced here: 220 us
  Pallas kernels  212 us (96%)
  other arithmetic  3.34 us (2%)
  local copies, waits for them, and re-layouts  2.43 us (1%)
    pallas_call x1, Pallas kernels, scatter_call(): pl.pallas_call(scatter_kernel, out_shape=(jax.ShapeDtypeStruct((2, D, PIE...  57.1 us
    pallas_call x1, Pallas kernels, gather_call(): pl.pallas_call(gather_kernel, out_shape=(jax.ShapeDtypeStruct((2, D, PIEC...  47.5 us
    pallas_call x1, Pallas kernels, attend_back_call(): pl.pallas_call(attend_back_kernel, out_shape=(jax.ShapeDtypeStruct((KV, H...  34.9 us
    pallas_call x1, Pallas kernels, attend_call(): pl.pallas_call(attend_kernel, out_shape=(jax.ShapeDtypeStruct((16, KV, T,...  33.4 us
    pallas_call x1, Pallas kernels, mlp_call(): pl.pallas_call(mlp_kernel, out_shape=(jax.ShapeDtypeStruct((2, D, PIECE),...  24.7 us
    pallas_call x1, Pallas kernels, post_call(): pl.pallas_call(post_kernel, out_shape=(jax.ShapeDtypeStruct((2, D, PIECE)...  7.37 us
    pallas_call x1, Pallas kernels, pre_call(): pl.pallas_call(pre_kernel, out_shape=(jax.ShapeDtypeStruct((KV, T, 128),...  5.44 us

profile of v1, /device:TPU:0, one launch (start us, length us, event | category | flops | bytes accessed | tf_op | source)
XLA Modules:
  0.0 220.5 jit_solution(4529687105783761955)
XLA Ops:
  0.6 0.0 copy-start
  0.7 0.6 copy-done
  1.3 1.2 pad_maximum_fusion.gains
  2.5 0.6 fusion.2
  4.4 0.7 fusion.1
  5.1 0.7 compare_select_fusion.1
  5.8 0.6 reshape.110.qstart
  6.4 0.6 reshape.109.qpos
  6.9 0.8 multiply_sine_fusion
  7.8 47.5 %gather_weights.1 = (bf16[2,576,128]{2,1,0:T(8,128)(2,1)}, bf16[2,576,128]{2,1,0:T(8,128)(2,1)}, bf16[4,4,2,256,576]{4,3,2,1,0:T(8,128)(2,1)}) custom-call(bf16[18,144]{1,0:T(8,128)(2,1)} %bitcast.49, bf16[6,144]{1,0:T(8,128)(2,1)} %bitcast.51, bf16[6,144]{1,0:T(8,128)(2,1)} %bitcast.52, bf16[18,144]{1,0:T(8,128)(2,1)} %bitcast.50, ...), custom_call_target="tpu_custom_call" | custom-call | tf_op jit(solution)/shard_map/gather_weights/pallas_call | solution.py:284
  55.3 5.4 %project_qkv.1 = (bf16[3,256,128]{2,1,0:T(8,128)(2,1)}, bf16[3,128,768]{2,1,0:T(8,128)(2,1)}, bf16[256,576]{1,0:T(8,128)(2,1)}) custom-call(bf16[32,256,576]{2,1,0:T(8,128)(2,1)} %bitcast.40, bf16[2,576,128]{2,1,0:T(8,128)(2,1)} %get-tuple-element.45.tok, f32[32,256]{1,0:T(8,128)} %get-tuple-element.100.cos, f32[32,256]{1,0:T(8,128)} %get-tuple-element.99.sin, ...), custom_call_target="tpu_custom_call" | custom-call | tf_op jit(solution)/shard_map/project_qkv/pallas_call | solution.py:363
  60.7 33.4 %attend_forward.1 = (bf16[16,3,256,128]{3,2,1,0:T(8,128)(2,1)}, f32[3,64,768]{2,1,0:T(8,128)}, f32[3,1,768]{2,1,0:T(1,128)}) custom-call(bf16[3,256,128]{2,1,0:T(8,128)(2,1)} %get-tuple-element.47.kv, bf16[3,128,768]{2,1,0:T(8,128)(2,1)} %get-tuple-element.48.qt, s32[1,768]{1,0:T(1,128)} %reshape.109.qpos, s32[1,768]{1,0:T(1,128)} %reshape.110.qstart), custom_call_target="tpu_custom_call" | custom-call | tf_op jit(solution)/shard_map/attend_forward/pallas_call | solution.py:548
  94.2 24.7 %feed_forward.1 = (bf16[2,576,128]{2,1,0:T(8,128)(2,1)}, f32[256,576]{1,0:T(8,128)}, bf16[3,128,768]{2,1,0:T(8,128)(2,1)}, f32[3,1,768]{2,1,0:T(1,128)}, bf16[32,256,576]{2,1,0:T(8,128)(2,1)}) custom-call(bf16[32,256,576]{2,1,0:T(8,128)(2,1)} %bitcast.41, bf16[2,576,128]{2,1,0:T(8,128)(2,1)} %get-tuple-element.45.tok, ...), custom_call_target="tpu_custom_call" | custom-call | tf_op jit(solution)/shard_map/feed_forward/pallas_call | solution.py:658
  118.9 34.9 %attend_backward.1 = (f32[3,64,768]{2,1,0:T(8,128)}, f32[3,256,128]{2,1,0:T(8,128)}) custom-call(bf16[16,3,256,128]{3,2,1,0:T(8,128)(2,1)} %get-tuple-element.52.kv, bf16[3,128,768]{2,1,0:T(8,128)(2,1)} %get-tuple-element.48.qt, bf16[3,128,768]{2,1,0:T(8,128)(2,1)} %get-tuple-element.53.dot, f32[3,1,768]{2,1,0:T(1,128)} %get-tuple-element.54.lse, ...), custom_call_target="tpu_custom_call" | custom-call | tf_op jit(solution)/shard_map/attend_backward/pallas_call | solution.py:819
  153.8 7.4 %project_back.1 = (bf16[2,576,128]{2,1,0:T(8,128)(2,1)}, bf16[32,256,576]{2,1,0:T(8,128)(2,1)}) custom-call(bf16[32,256,576]{2,1,0:T(8,128)(2,1)} %get-tuple-element.50.dw_in, bf16[32,256,576]{2,1,0:T(8,128)(2,1)} %bitcast.42, bf16[2,576,128]{2,1,0:T(8,128)(2,1)} %get-tuple-element.45.tok, ...), custom_call_target="tpu_custom_call", output_to_operand_aliasing={{1}: (0, {})} | custom-call | tf_op jit(solution)/shard_map/project_back/pallas_call | solution.py:891
  161.2 57.1 %scatter_grads.1 = (bf16[2,576,128]{2,1,0:T(8,128)(2,1)}, bf16[2,576,128]{2,1,0:T(8,128)(2,1)}, f32[160,144]{1,0:T(8,128)}, f32[32,384]{1,0:T(8,128)}) custom-call(bf16[4,4,2,256,576]{4,3,2,1,0:T(8,128)(2,1)} %bitcast.43, bf16[2,576,128]{2,1,0:T(8,128)(2,1)} %get-tuple-element.60.mixed, bf16[2,576,128]{2,1,0:T(8,128)(2,1)} %get-tuple-element.61.tgrad), custom_call_target="tpu_custom_call" | custom-call | tf_op jit(solution)/shard_map/scatter_grads/pallas_call | solution.py:1110
  218.3 2.0 write_outputs.1
  (5 shorter events, 0.0 us)
Async XLA Ops:
  0.6 0.7 copy-start

commit v2 on v0

v2 whole, which is shorter than its diff:
```python
import numpy as np
import ml_dtypes
import jax
import jax.numpy as jnp
from jax import lax
from jax.experimental import pallas as pl
from jax.experimental.pallas import tpu as pltpu
from jax.sharding import PartitionSpec as P

D = 576
HEADS = 9
KV = 3
HD = 64
FF = 1536
PIECE = 128
T = 2 * PIECE
LANES = 3 * T
EPS = 1e-05
THETA = 100000.0
MASKED = -1e30
MESH = pl.DeviceIdType.MESH
F32 = jnp.float32
BF16 = jnp.bfloat16
VLIMIT = 58 * 1024 * 1024


def spread_matrix():
    m = np.zeros((960, 1024), np.float32)
    n = np.arange(576)
    m[n, 32 * (n // 18) + n % 18] = 1
    n = np.arange(192)
    m[576 + n, 32 * (n // 6) + 18 + n % 6] = 1
    m[768 + n, 32 * (n // 6) + 24 + n % 6] = 1
    return m.astype(ml_dtypes.bfloat16)


def gain_matrix():
    n = np.arange(576)
    fold = np.zeros((576, 576), np.float32)
    for b in range(4):
        fold[n, 144 * b + n % 18] = 1
    owner = (n[None, :] // 18 == np.arange(32)[:, None]).astype(np.float32)
    return fold.astype(ml_dtypes.bfloat16), owner


def nn(a, b):
    return lax.dot_general(a, b, (((1,), (0,)), ((), ())), preferred_element_type=F32)


def nt(a, b):
    return lax.dot_general(a, b, (((1,), (1,)), ((), ())), preferred_element_type=F32)


def tn(a, b):
    return lax.dot_general(a, b, (((0,), (0,)), ((), ())), preferred_element_type=F32)


def rcopy(src, dst, ss, rs, dev):
    return pltpu.make_async_remote_copy(
        src_ref=src, dst_ref=dst, send_sem=ss, recv_sem=rs, device_id=dev, device_id_type=MESH
    )


def place():
    b = lax.axis_index("batch")
    s = lax.axis_index("seq")
    c = lax.rem(s, 2)
    p = lax.div(s, 2)
    return b, s, c, p, lax.div(p, 4), lax.rem(p, 4)


def seq_of(y, x, c):
    return (y * 4 + x) * 2 + c


def hop(i, d):
    return lax.rem(i + d, 4)


def hail(devices):
    bar = pltpu.get_barrier_semaphore()
    for dev in devices:
        pl.semaphore_signal(bar, inc=1, device_id=dev, device_id_type=MESH)
    return bar


def neighbours(b, s, c, y, x):
    found = [(b, seq_of(y, x, 1 - c))]
    for d in (1, 3):
        found += [
            (hop(b, d), s),
            (b, seq_of(y, hop(x, d), c)),
            (b, seq_of(hop(y, d), x, c)),
        ]
    return found


class Ring:
    def __init__(self, dev, ss, rs):
        self.dev, self.ss, self.rs = dev, ss, rs

    def copy(self, n, src, dst):
        du, dv = {0: (1, 0), 1: (3, 0), 2: (1, 0), 3: (3, 0)}.get(n, (0, 1 if n // 4 in (1, 3) else 3))
        return rcopy(src, dst, self.ss.at[n], self.rs.at[n], self.dev(du, dv))


def token_rows(ref):
    return jnp.concatenate([ref[0].astype(F32).T, ref[1].astype(F32).T], axis=0)


def gain_row(blocks, row, fold, owner):
    at = lax.broadcasted_iota(jnp.int32, (32, 1024), 0) * 32 + row
    one = (lax.broadcasted_iota(jnp.int32, (32, 1024), 1) == at).astype(F32).astype(BF16)
    spread = nt(nn(one, blocks[:, 0:128]).astype(BF16), fold[:, 0:128])
    return jnp.sum(spread * owner, axis=0, keepdims=True)


def place_row(row, values):
    at = lax.broadcasted_iota(jnp.int32, (1024, 32), 1) * 32 + row
    one = (lax.broadcasted_iota(jnp.int32, (1024, 32), 0) == at).astype(F32).astype(BF16)
    return nn(one, values.astype(BF16))


def diagonal_mask(p, qpos, qstart):
    row = lax.broadcasted_iota(jnp.int32, (T, 1), 0)
    kpos = jnp.where(row < PIECE, p * PIECE + row, (31 - p) * PIECE + row - PIECE)
    return (kpos <= qpos) & (kpos >= qstart)


def first_mask(qstart):
    row = lax.broadcasted_iota(jnp.int32, (PIECE, 1), 0)
    return row >= qstart


def pick(i, values):
    found = values[0]
    for k, value in enumerate(values[1:]):
        found = jnp.where(i == k + 1, value, found)
    return found


FORWARD = ((0, 0), (3, 0), (1, 0), (0, 3), (0, 1), (2, 0), (3, 3), (3, 1), (1, 3), (1, 1), (2, 3), (2, 1), (0, 2), (3, 2), (1, 2), (2, 2))
BACKWARD = ((0, 0), (2, 2), (1, 2), (3, 2), (0, 2), (2, 1), (2, 3), (1, 1), (1, 3), (3, 1), (3, 3), (0, 1), (0, 3), (2, 0), (1, 0), (3, 0))
HALVES = (pl.ds(0, PIECE), pl.ds(PIECE, PIECE))


ROWS = 224


class Plane:
    def __init__(self):
        self.b, self.s, self.c, self.p, self.y, self.x = place()
        c, y, x = self.c, self.y, self.x
        self.u, self.v = jnp.where(c == 0, x, y), jnp.where(c == 0, y, x)
        self.su, self.sv = 1 + 3 * c, 4 - 3 * c
        self.other = (self.b, seq_of(y, x, 1 - c))

    def index(self, du, dv):
        return lax.rem(self.u + du, 4) * self.su + lax.rem(self.v + dv, 4) * self.sv

    def dev(self, du, dv):
        return (self.b, 2 * self.index(du, dv) + self.c)

    def common(self, du, dv):
        return du * self.su + dv * self.sv


class Gather:
    def __init__(self, plane, view, own, sems, swap=None):
        self.ring = Ring(plane.dev, sems.at[0], sems.at[1])
        self.view, self.own, self.swap = view, own, swap
        self.later = []

    def copy(self, n, du, dv, part=None):
        ref = self.view(du, dv, part)
        return self.ring.copy(n, self.own if (du, dv) == (0, 0) else ref, ref)

    def send(self, *item):
        self.copy(*item).start()
        self.later.append(item)

    def arrive(self, n, du, dv, part=None):
        ref = self.view(du, dv, part)
        self.ring.copy(n, ref, ref).wait_recv()

    def done(self, du, dv):
        if self.swap is not None:
            self.swap(du, dv).start()

    def begin_u(self):
        self.send(0, 0, 0)
        self.send(1, 0, 0)

    def begin_v(self):
        self.send(4, 0, 0)
        self.send(8, 0, 0)
        self.done(0, 0)

    def near(self):
        for n, du in ((0, 3), (1, 1)):
            self.arrive(n, du, 0)
            self.send(2 + n, du, 0, n)
            self.send(4 + du, du, 0)
            self.send(8 + du, du, 0)
            self.done(du, 0)

    def far(self):
        self.arrive(2, 2, 0, 0)
        self.arrive(3, 2, 0, 1)
        self.send(6, 2, 0)
        self.send(10, 2, 0)
        self.done(2, 0)

    def line(self, w):
        self.arrive(4 + w, w, 3)
        self.send(12 + w, w, 3, 0)
        self.done(w, 3)
        self.arrive(8 + w, w, 1)
        self.send(16 + w, w, 1, 1)
        self.done(w, 1)

    def last(self, w):
        self.arrive(12 + w, w, 2, 0)
        self.arrive(16 + w, w, 2, 1)
        self.done(w, 2)

    def finish(self):
        for item in self.later:
            self.copy(*item).wait_send()
        if self.swap is not None:
            for du in range(4):
                for dv in range(4):
                    self.swap(du, dv).wait()


class Reduce:
    def __init__(self, plane, view, add, bufs, sems):
        self.ring = Ring(plane.dev, sems.at[0], sems.at[1])
        self.view, self.add = view, add
        va, vb, vp, vm, ua, ub, up, um = bufs
        self.pieces = {
            2: (2, 0, 0, ua), 3: (2, 0, 1, ub), 0: (1, 0, None, up), 1: (3, 0, None, um),
        }
        for w in range(4):
            self.pieces[12 + w] = (w, 2, 0, va.at[w])
            self.pieces[16 + w] = (w, 2, 1, vb.at[w])
            self.pieces[4 + w] = (w, 1, None, vp.at[w])
            self.pieces[8 + w] = (w, 3, None, vm.at[w])

    def copy(self, n):
        du, dv, part, dst = self.pieces[n]
        return self.ring.copy(n, self.view(du, dv, part), dst)

    def take(self, n, du, dv, part=None):
        self.copy(n).wait_recv()
        self.add(du, dv, part, self.pieces[n][3])

    def event(self, du, dv):
        if dv == 2:
            self.copy(12 + du).start()
            self.copy(16 + du).start()
        elif dv == 1:
            self.take(12 + du, du, 1, 0)
            self.copy(4 + du).start()
        elif dv == 3:
            self.take(16 + du, du, 3, 1)
            self.copy(8 + du).start()
        else:
            self.take(4 + du, du, 0)
            self.take(8 + du, du, 0)
            if du == 2:
                self.copy(2).start()
                self.copy(3).start()
            elif du == 1:
                self.take(2, 1, 0, 0)
                self.copy(0).start()
            elif du == 3:
                self.take(3, 3, 0, 1)
                self.copy(1).start()

    def end(self):
        self.take(0, 0, 0)
        self.take(1, 0, 0)

    def finish(self):
        for n in self.pieces:
            self.copy(n).wait_send()


class SumZ:
    def __init__(self, b, s, items, sems):
        self.b, self.s, self.items, self.sems = b, s, items, sems

    def copies(self, n):
        at = hop(self.b, 2 if n > 1 else 1 + 2 * n)
        dev = (hop(self.b, 1 if n in (0, 2) else 3), self.s)
        found = []
        for k, (ref, bufs) in enumerate(self.items):
            size = ref.shape[1] // 2
            src = ref.at[at] if n < 2 else ref.at[at, pl.ds(size * (n - 2), size)]
            found.append(rcopy(src, bufs[n], self.sems.at[0, k, n], self.sems.at[1, k, n], dev))
        return found

    def start(self, n):
        for cp in self.copies(n):
            cp.start()

    def begin(self):
        self.start(2)
        self.start(3)

    def middle(self):
        for n in (2, 3):
            for cp in self.copies(n):
                cp.wait_recv()
            at = hop(self.b, 1 if n == 2 else 3)
            for ref, bufs in self.items:
                size = ref.shape[1] // 2
                part = (at, pl.ds(size * (n - 2), size))
                ref[part] = ref[part] + bufs[n][...]
            self.start(n - 2)

    def result(self):
        for n in (0, 1):
            for cp in self.copies(n):
                cp.wait_recv()
        found = []
        for ref, bufs in self.items:
            found.append(ref[self.b].astype(F32) + bufs[0][...].astype(F32) + bufs[1][...].astype(F32))
        return found

    def finish(self):
        for n in range(4):
            for cp in self.copies(n):
                cp.wait_send()


SCRATCH = {
    "spread": ((960, 1024), BF16), "sprt": ((1024, 960), BF16), "fold": ((D, D), BF16),
    "raw_f": ((160, 144), F32), "dwn_f": ((32, 384), F32),
    "za": ((4, 160, 144), BF16), "zd": ((4, 32, 384), BF16),
    "blk1": ((32, D), BF16), "blk2": ((ROWS, D), BF16),
    "g1": ((32, 32, D), BF16), "g2": ((32, ROWS, D), BF16),
    "tok": ((2, D, PIECE), BF16), "cot": ((2, D, PIECE), BF16),
    "gain_s": ((4, 8, D), F32), "x_s": ((T, D), F32), "h1": ((T, D), BF16),
    "kv": ((KV, T, 128), BF16), "qt": ((KV, 128, LANES), BF16), "dot": ((KV, 128, LANES), BF16),
    "kva": ((16, KV, T, 128), BF16),
    "m_s": ((KV, 1, LANES), F32), "l_s": ((KV, 1, LANES), F32), "delta": ((KV, 1, LANES), F32),
    "acc": ((KV, HD, LANES), F32), "dq": ((KV, HD, LANES), F32), "dkv": ((KV, T, 128), F32),
    "wd_s": ((D, FF), BF16), "act_s": ((T, FF), BF16), "wo_s": ((D, D), BF16),
    "h2_s": ((T, D), BF16), "dh2_s": ((T, D), F32), "mix_s": ((T, D), F32),
    "mixed": ((2, D, PIECE), BF16), "tgrad": ((2, D, PIECE), BF16),
    "sent": ((16, KV, T, 128), BF16),
    "kva_": ((4, KV, PIECE, 128), BF16), "kvb_": ((4, KV, PIECE, 128), BF16),
    "kvp_": ((4, KV, T, 128), BF16), "kvm_": ((4, KV, T, 128), BF16),
    "kua_": ((KV, PIECE, 128), BF16), "kub_": ((KV, PIECE, 128), BF16),
    "kup_": ((KV, T, 128), BF16), "kum_": ((KV, T, 128), BF16),
    "r2": ((16, ROWS, D), BF16),
    "wva": ((4, ROWS // 2, D), BF16), "wvb": ((4, ROWS // 2, D), BF16),
    "wvp": ((4, ROWS, D), BF16), "wvm": ((4, ROWS, D), BF16),
    "wua": ((ROWS // 2, D), BF16), "wub": ((ROWS // 2, D), BF16),
    "wup": ((ROWS, D), BF16), "wum": ((ROWS, D), BF16),
    "r1": ((16, 32, D), BF16),
    "ava": ((4, 16, D), BF16), "avb": ((4, 16, D), BF16),
    "avp": ((4, 32, D), BF16), "avm": ((4, 32, D), BF16),
    "aua": ((16, D), BF16), "aub": ((16, D), BF16),
    "aup": ((32, D), BF16), "aum": ((32, D), BF16),
    "zs2": ((4, 128, 144), BF16), "zd2": ((4, 32, 384), BF16), "zs1": ((4, 32, 144), BF16),
    "zs2p": ((128, 144), BF16), "zs2m": ((128, 144), BF16), "zs2a": ((64, 144), BF16), "zs2b": ((64, 144), BF16),
    "zd2p": ((32, 384), BF16), "zd2m": ((32, 384), BF16), "zd2a": ((16, 384), BF16), "zd2b": ((16, 384), BF16),
    "zs1p": ((32, 144), BF16), "zs1m": ((32, 144), BF16), "zs1a": ((16, 144), BF16), "zs1b": ((16, 144), BF16),
}
SEMS = {
    "lsem": (4,), "zsem": (2, 2, 4), "zz": (4, 2, 2), "zl": (4,),
    "g1sem": (2, 20), "g1swap": (2, 16), "g2sem": (2, 20), "g2swap": (2, 16), "kvsem": (2, 20),
    "dksem": (2, 20), "d2fold": (2, 16), "d2sem": (2, 20), "d1fold": (2, 16), "d1sem": (2, 20),
    "z2sem": (2, 2, 4), "z1sem": (2, 1, 4),
}
INPUTS = (
    "wq", "wk", "wv", "wo", "wg", "wu", "wd", "gains", "tokens", "cotin", "cos", "sin", "qpos", "qstart",
    "owner", "spread_in", "sprt_in", "fold_in",
)
OUTPUTS = ("mixed_o", "tgrad_o", "raw_o", "down_o")


class Refs:
    def __init__(self, refs):
        for name, ref in zip((*INPUTS, *OUTPUTS, *SCRATCH, *SEMS), refs, strict=True):
            setattr(self, name, ref)


def layer_kernel(*refs):
    r = Refs(refs)
    plane = Plane()
    b, s, c, p, y, x = plane.b, plane.s, plane.c, plane.p, plane.y, plane.x
    early = jnp.minimum(s, 31 - s)
    slot = lax.div(s, 16)
    bar = hail(neighbours(b, s, c, y, x))
    around = [2 * early, 2 * early + 1, p, 31 - p]
    for peer in around:
        @pl.when(peer != s)
        def _():
            pl.semaphore_signal(bar, inc=1, device_id=(b, peer), device_id_type=MESH)
    constants = [
        pltpu.make_async_copy(src, dst, r.lsem.at[k])
        for k, (src, dst) in enumerate(((r.spread_in, r.spread), (r.sprt_in, r.sprt), (r.fold_in, r.fold)))
    ]
    for cp in constants:
        cp.start()
    r.raw_f[...] = jnp.zeros_like(r.raw_f)
    r.dwn_f[...] = jnp.zeros_like(r.dwn_f)
    for at, ref in ((0, r.wq), (18, r.wk), (24, r.wv), (32, r.wo), (64, r.wg), (112, r.wu)):
        r.raw_f[at : at + ref.shape[0], :] = ref[...].astype(F32)
    r.raw_f[30:32, 0:18] = r.gains[...].astype(F32)
    r.dwn_f[0:18, :] = r.wd[...].astype(F32)
    r.za[pl.ds(b, 1)] = r.raw_f[...].astype(BF16)[None]
    r.zd[pl.ds(b, 1)] = r.dwn_f[...].astype(BF16)[None]
    peers = 7
    for peer in around:
        peers = peers + jnp.where(peer != s, 1, 0)
    pl.semaphore_wait(bar, peers)

    def zcopies(n, at, part):
        dev = (hop(b, 1 if n in (0, 2) else 3), s)
        found = []
        for k, (ref, rows) in enumerate(((r.za, 80), (r.zd, 16))):
            view = ref.at[at] if part is None else ref.at[at, pl.ds(rows * part, rows)]
            found.append(rcopy(view, view, r.zsem.at[0, k, n], r.zsem.at[1, k, n], dev))
        return found

    def start(copies):
        for cp in copies:
            cp.start()

    zsent = [zcopies(0, b, None), zcopies(1, b, None)]
    start(zsent[0] + zsent[1])

    def outward(k, src_ref, dst_ref, act_remote, act_local):
        for m in (0, 1):
            dst = 2 * early + m

            @pl.when(dst != s)
            def _():
                act_remote(rcopy(src_ref.at[m], dst_ref.at[slot], r.zz.at[k, 0, m], r.zz.at[k, 1, slot], (b, dst)))

            @pl.when(dst == s)
            def _():
                act_local(pltpu.make_async_copy(src_ref.at[m], dst_ref.at[slot], r.zl.at[k]))

    def outward_wait(k, src_ref, dst_ref):
        for q, src in enumerate((p, 31 - p)):
            @pl.when(src != s)
            def _():
                rcopy(src_ref.at[0], dst_ref.at[q], r.zz.at[k, 0, 0], r.zz.at[k, 1, q], (b, src)).wait_recv()

    def homeward(k, src_ref, dst_ref, act_remote, act_local):
        for q, dst in enumerate((p, 31 - p)):
            @pl.when(dst != s)
            def _():
                act_remote(rcopy(src_ref.at[q], dst_ref.at[c], r.zz.at[k, 0, q], r.zz.at[k, 1, c], (b, dst)))

            @pl.when(dst == s)
            def _():
                act_local(pltpu.make_async_copy(src_ref.at[q], dst_ref.at[c], r.zl.at[k]))

    def homeward_wait(k, src_ref, dst_ref):
        for m in (0, 1):
            src = 2 * early + m

            @pl.when(src != s)
            def _():
                rcopy(src_ref.at[0], dst_ref.at[m], r.zz.at[k, 0, 0], r.zz.at[k, 1, m], (b, src)).wait_recv()

    begin = (lambda cp: cp.start(), lambda cp: cp.start())
    ended = (lambda cp: cp.wait_send(), lambda cp: cp.wait())
    outward(0, r.tokens, r.tok, *begin)
    outward(1, r.cotin, r.cot, *begin)

    for n, way in ((0, 3), (1, 1)):
        for cp in zcopies(n, hop(b, way), None):
            cp.wait_recv()
        zsent.append(zcopies(2 + n, hop(b, way), n))
        start(zsent[-1])
    for n in (2, 3):
        for cp in zcopies(n, hop(b, 2), n - 2):
            cp.wait_recv()
    main = jnp.concatenate([r.za[i].astype(F32) for i in range(4)], axis=1).astype(BF16)
    r.blk1[...] = main[0:32]

    def weights(ref, own, sems, swap_sems, half):
        def view(du, dv, part=None):
            at = 2 * plane.index(du, dv) + c
            return ref.at[at] if part is None else ref.at[at, pl.ds(half * part, half)]

        def swap(du, dv):
            n = plane.common(du, dv)
            dst = view(du, dv)
            src = own if (du, dv) == (0, 0) else dst
            return rcopy(src, dst, swap_sems.at[0, n], swap_sems.at[1, n], plane.other)

        return Gather(plane, view, own, sems, swap)

    first = weights(r.g1, r.blk1, r.g1sem, r.g1swap, 16)
    second = weights(r.g2, r.blk2, r.g2sem, r.g2swap, ROWS // 2)
    first.begin_u()
    first.begin_v()
    r.g1[pl.ds(s, 1)] = r.blk1[...][None]
    down = jnp.concatenate([r.zd[i] for i in range(4)], axis=1)
    r.blk2[0:128, :] = main[32:160]
    r.blk2[128:224, 512:576] = jnp.zeros((96, 64), BF16)
    for k in range(3):
        r.blk2[128 + 32 * k : 160 + 32 * k, 0:512] = down[:, 512 * k : 512 * (k + 1)]
    first.near()
    second.begin_u()
    r.g2[pl.ds(s, 1)] = r.blk2[...][None]
    first.line(0)
    first.far()
    outward_wait(0, r.tokens, r.tok)
    outward(0, r.tokens, r.tok, *ended)
    r.x_s[...] = token_rows(r.tok)
    for w in (3, 1, 2):
        first.line(w)
    second.begin_v()
    for w in (0, 3, 1, 2):
        first.last(w)
    first.finish()
    for cp in constants:
        cp.wait()

    owner_rows = r.owner[...]
    fold = r.fold[...]
    wa = r.g1[...].reshape(1024, D)
    gain1 = gain_row(wa, 30, fold, owner_rows)
    r.gain_s[0] = jnp.broadcast_to(gain1, (8, D))
    r.gain_s[1] = jnp.broadcast_to(gain_row(wa, 31, fold, owner_rows), (8, D))
    xin = r.x_s[...]
    inv1 = lax.rsqrt(jnp.sum(xin * xin, axis=-1, keepdims=True) * (1.0 / D) + EPS)
    r.h1[...] = (xin * inv1 * gain1).astype(BF16)
    w_all = nn(r.spread[...], wa).astype(BF16)
    z = nt(w_all, r.h1[...])
    co, si = r.cos[...], r.sin[...]

    def rot(a):
        a1, a2 = a[0:32], a[32:64]
        return jnp.concatenate([a1 * co - a2 * si, a2 * co + a1 * si], axis=0)

    def unrot(a):
        a1, a2 = a[0:32], a[32:64]
        return jnp.concatenate([a1 * co + a2 * si, a2 * co - a1 * si], axis=0)

    for h in range(KV):
        kh = rot(z[576 + 64 * h : 640 + 64 * h])
        vh = z[768 + 64 * h : 832 + 64 * h]
        r.kv[h] = jnp.concatenate([kh, vh], axis=0).T.astype(BF16)

    def kview(ref):
        def view(du, dv, part=None):
            at = plane.index(du, dv)
            return ref.at[at] if part is None else ref.at[at, :, HALVES[part]]
        return view

    keys = Gather(plane, kview(r.kva), r.kv, r.kvsem)
    keys.begin_u()
    keys.begin_v()
    r.kva[pl.ds(p, 1)] = r.kv[...][None]
    for h in range(HEADS):
        q = (rot(z[64 * h : 64 * h + 64]).astype(BF16).astype(F32) * 0.125).astype(BF16)
        kvh, gi = h // 3, h % 3
        for piece in range(2):
            lane = piece * 384 + gi * 128
            r.qt[kvh, 0:64, lane : lane + 128] = q[:, piece * 128 : piece * 128 + 128]
    for h in range(KV):
        r.qt[h, 64:128, :] = jnp.zeros((64, LANES), BF16)
        r.dot[h, 0:64, :] = jnp.zeros((64, LANES), BF16)

    r.m_s[...] = jnp.full_like(r.m_s, MASKED)
    r.l_s[...] = jnp.zeros_like(r.l_s)
    r.acc[...] = jnp.zeros_like(r.acc)
    every = pl.ds(0, LANES)
    late = pl.ds(384, 384)

    def step(block, h, lanes, mask, drop):
        st = nn(block, r.qt[h, :, lanes])
        if mask is not None:
            st = jnp.where(mask, st, MASKED)
        m_old = r.m_s[h, :, lanes]
        top = jnp.max(st, axis=0, keepdims=True)
        if drop is None:
            m_new = jnp.maximum(m_old, top)
            m_sub = m_new
        else:
            m_new = jnp.maximum(m_old, jnp.where(drop, MASKED, top))
            m_sub = jnp.where(drop, -MASKED, m_new)
        pt = jnp.exp(st - m_sub)
        a = jnp.exp(m_old - m_new)
        r.m_s[h, :, lanes] = m_new
        r.l_s[h, :, lanes] = r.l_s[h, :, lanes] * a + jnp.sum(pt, axis=0, keepdims=True)
        r.acc[h, :, lanes] = r.acc[h, :, lanes] * a + tn(block, pt.astype(BF16))[64:128]

    def allowed():
        return diagonal_mask(p, r.qpos[...], r.qstart[...])

    mask = allowed()
    for h in range(KV):
        step(r.kv[h], h, every, mask, None)

    events = {
        1: [keys.near, second.near], 2: [lambda: keys.line(0)], 3: [keys.far, lambda: second.line(0)],
        4: [lambda: keys.line(3)], 5: [lambda: keys.line(1), second.far], 7: [lambda: keys.line(2)],
        8: [lambda: second.line(3)], 10: [lambda: second.line(1)],
        12: [lambda: keys.last(0), lambda: second.line(2)], 13: [lambda: keys.last(3)],
        14: [lambda: keys.last(1), lambda: second.last(0)], 15: [lambda: keys.last(2)],
    }

    def visit(i, carry):
        for k, todo in events.items():
            @pl.when(i == k)
            def _():
                for event in todo:
                    event()

        j = plane.index(pick(i, [o[0] for o in FORWARD]), pick(i, [o[1] for o in FORWARD]))

        @pl.when((j < p) & (j > 0))
        def _():
            for h in range(KV):
                step(r.kva[j, h, 0:PIECE, :], h, every, None, None)

        @pl.when((j < p) & (j == 0))
        def _():
            keep = first_mask(r.qstart[...])
            for h in range(KV):
                step(r.kva[0, h, 0:PIECE, :], h, every, keep, None)

        @pl.when(j > p)
        def _():
            drop = r.qstart[:, late] >= PIECE
            for h in range(KV):
                step(r.kva[j, h], h, late, None, drop)

        return carry

    lax.fori_loop(1, 16, visit, 0)
    for h in range(KV):
        total = r.l_s[h]
        r.acc[h] = r.acc[h] / total
        r.m_s[h] = r.m_s[h] + jnp.log(total)
    rows = []
    for h in range(HEADS):
        kvh, gi = h // 3, h % 3
        rows.append(
            jnp.concatenate(
                [r.acc[kvh, :, q * 384 + gi * 128 : q * 384 + gi * 128 + 128] for q in range(2)], axis=1
            )
        )
    att_t = jnp.concatenate(rows, axis=0).T.astype(BF16)
    outward_wait(1, r.cotin, r.cot)
    outward(1, r.cotin, r.cot, *ended)
    dy = token_rows(r.cot).astype(BF16)
    dyt_rows = jnp.concatenate([r.cot[0], r.cot[1]], axis=1)
    for w in (3, 1, 2):
        second.last(w)
    keys.finish()
    second.finish()
    for group in zsent:
        for cp in group:
            cp.wait_send()

    p2 = r.spread[0:576, :]
    p2t = r.sprt[:, 0:576]
    r.wo_s[...] = nn(p2, r.g2[:, 0:32, :].reshape(1024, D)).astype(BF16)
    for k in range(3):
        third = r.g2[:, 128 + 32 * k : 160 + 32 * k, 0:512].reshape(1024, 512)
        r.wd_s[:, 512 * k : 512 * k + 512] = nn(p2, third).astype(BF16)
    middle = r.x_s[...] + nt(att_t, r.wo_s[...])
    inv2 = lax.rsqrt(jnp.sum(middle * middle, axis=-1, keepdims=True) * (1.0 / D) + EPS)
    n2 = middle * inv2
    r.h2_s[...] = (n2 * r.gain_s[1, 0:1, :]).astype(BF16)
    r.mix_s[...] = middle
    r.dh2_s[...] = jnp.zeros_like(r.dh2_s)

    def chunk(f, carry):
        at = pl.ds(8 * f, 8)
        lanes = pl.ds(pl.multiple_of(384 * f, 128), 384)
        wg = r.g2[at, 32:80, :].reshape(384, D)
        wu = r.g2[at, 80:128, :].reshape(384, D)
        h2 = r.h2_s[...]
        gate = nt(h2, wg)
        up = nt(h2, wu)
        sig = 1.0 / (1.0 + jnp.exp(-gate))
        silu = gate * sig
        act = (silu * up).astype(BF16)
        r.act_s[:, lanes] = act
        wdf = r.wd_s[:, lanes]
        r.mix_s[...] += nt(act, wdf)
        da = nn(dy, wdf)
        dup = (da * silu).astype(BF16)
        dgate = (da * up * sig * (1.0 + gate * (1.0 - sig))).astype(BF16)
        r.dh2_s[...] += nn(dgate, wg) + nn(dup, wu)
        r.g2[at, 32:80, :] = tn(dgate, h2).astype(BF16).reshape(8, 48, D)
        r.g2[at, 80:128, :] = tn(dup, h2).astype(BF16).reshape(8, 48, D)
        return carry

    lax.fori_loop(0, 4, chunk, 0)
    for q in range(2):
        r.mixed[q] = r.mix_s[PIECE * q : PIECE * (q + 1), :].T.astype(BF16)
    homeward(2, r.mixed, r.mixed_o, *begin)
    dyt = nn(p2t, dyt_rows).astype(BF16)
    r.g2[:, 128:224, 512:576] = jnp.zeros((32, 96, 64), BF16)
    for k in range(3):
        part = nn(dyt, r.act_s[:, 512 * k : 512 * k + 512]).astype(BF16)
        r.g2[:, 128 + 32 * k : 160 + 32 * k, 0:512] = part.reshape(32, 32, 512)
    dh2 = r.dh2_s[...]
    gsum = jnp.sum(dh2 * n2, axis=0, keepdims=True)
    r.gain_s[2] = jnp.broadcast_to(gsum, (8, D))
    gain = nn((jnp.concatenate([r.gain_s[2]] * 4, axis=0) * r.owner[...]).astype(BF16), r.fold[...])
    g2v = dh2 * r.gain_s[1, 0:1, :]
    dmid = dy.astype(F32) + inv2 * (g2v - n2 * (jnp.sum(g2v * n2, axis=-1, keepdims=True) * (1.0 / D)))
    r.mix_s[...] = dmid
    dbt = nn(p2t, dmid.T.astype(BF16)).astype(BF16)
    r.g2[:, 0:32, :] = (nn(dbt, att_t) + place_row(18, gain)).astype(BF16).reshape(32, 32, D)

    def folder(ref, land, sems):
        def copy(du, dv):
            at = plane.index(du, dv)
            n = plane.common(du, dv)
            return rcopy(ref.at[2 * at + 1 - c], land.at[at], sems.at[0, n], sems.at[1, n], plane.other)

        def fold_in(du, dv):
            copy(du, dv).wait_recv()
            at = plane.index(du, dv)
            ref[2 * at + c] = ref[2 * at + c] + land[at]

        return copy, fold_in

    def reducer(ref, bufs, sems, half):
        def view(du, dv, part=None):
            at = 2 * plane.index(du, dv) + c
            return ref.at[at] if part is None else ref.at[at, pl.ds(half * part, half)]

        def add(du, dv, part, buf):
            at = 2 * plane.index(du, dv) + c
            where = (at,) if part is None else (at, pl.ds(half * part, half))
            ref[where] = ref[where] + buf[...]

        return Reduce(plane, view, add, bufs, sems)

    copy2, fold2 = folder(r.g2, r.r2, r.d2fold)
    sum2 = reducer(r.g2, (r.wva, r.wvb, r.wvp, r.wvm, r.wua, r.wub, r.wup, r.wum), r.d2sem, ROWS // 2)
    order = BACKWARD[1:] + BACKWARD[:1]
    for du, dv in order:
        copy2(dv, du).start()
    datt = nn(dmid.astype(BF16), r.wo_s[...]).astype(BF16).astype(F32).T
    for h in range(HEADS):
        kvh, gi = h // 3, h % 3
        for q in range(2):
            lane = q * 384 + gi * 128
            part = datt[64 * h : 64 * h + 64, 128 * q : 128 * q + 128]
            r.dot[kvh, 64:128, lane : lane + 128] = part.astype(BF16)
            r.delta[kvh, :, lane : lane + 128] = jnp.sum(
                part * r.acc[kvh, :, lane : lane + 128], axis=0, keepdims=True
            )

    def add_keys(du, dv, part, buf):
        at = plane.index(du, dv)
        if part is None:
            r.sent[at] = r.sent[at] + buf[...]
        else:
            rows = slice(PIECE * part, PIECE * (part + 1))
            r.sent[at, :, rows, :] = r.sent[at, :, rows, :] + buf[...]

    sumk = Reduce(
        plane, kview(r.sent), add_keys,
        (r.kva_, r.kvb_, r.kvp_, r.kvm_, r.kua_, r.kub_, r.kup_, r.kum_), r.dksem,
    )
    r.dq[...] = jnp.zeros_like(r.dq)

    def back(block, h, lanes, mask, drop):
        q = r.qt[h, :, lanes]
        do = r.dot[h, :, lanes]
        st = nn(block, q)
        if mask is not None:
            st = jnp.where(mask, st, MASKED)
        base = r.m_s[h, :, lanes]
        if drop is not None:
            base = jnp.where(drop, -MASKED, base)
        pt = jnp.exp(st - base)
        dp = nn(block, do)
        ds = (pt * (dp - r.delta[h, :, lanes])).astype(BF16)
        r.dq[h, :, lanes] += tn(block, ds)[0:64]
        return nt(ds, q) + nt(pt.astype(BF16), do)

    def visit_back(i, carry):
        j = plane.index(pick(i, [o[0] for o in BACKWARD]), pick(i, [o[1] for o in BACKWARD]))

        @pl.when(j < p)
        def _():
            r.sent[j, :, PIECE:T, :] = jnp.zeros((KV, PIECE, 128), BF16)

        @pl.when((j < p) & (j > 0))
        def _():
            for h in range(KV):
                r.sent[j, h, 0:PIECE, :] = back(r.kva[j, h, 0:PIECE, :], h, every, None, None).astype(BF16)

        @pl.when((j < p) & (j == 0))
        def _():
            keep = first_mask(r.qstart[...])
            for h in range(KV):
                r.sent[0, h, 0:PIECE, :] = back(r.kva[0, h, 0:PIECE, :], h, every, keep, None).astype(BF16)

        @pl.when(j > p)
        def _():
            drop = r.qstart[:, late] >= PIECE
            for h in range(KV):
                r.sent[j, h] = back(r.kva[j, h], h, late, None, drop).astype(BF16)

        for k, offset in enumerate(BACKWARD):
            if k:
                @pl.when(i == k)
                def _():
                    sumk.event(*offset)
                    fold2(*offset)
                    sum2.event(*offset)

        return carry

    lax.fori_loop(1, 16, visit_back, 0)
    mask = allowed()
    for h in range(KV):
        r.dkv[h] = back(r.kva[p, h], h, every, mask, None)
    for n, buf in ((4, r.kvp_.at[0]), (8, r.kvm_.at[0]), (0, r.kup_), (1, r.kum_)):
        sumk.copy(n).wait_recv()
        r.dkv[...] += buf[...].astype(F32)

    fold2(0, 0)
    sum2.event(0, 0)
    parts, vals = [], []
    for h in range(HEADS):
        kvh, gi = h // 3, h % 3
        part = jnp.concatenate(
            [r.dq[kvh, :, q * 384 + gi * 128 : q * 384 + gi * 128 + 128] for q in range(2)], axis=1
        )
        parts.append(unrot(part * 0.125))
    for h in range(KV):
        both = r.dkv[h].T
        parts.append(unrot(both[0:64]))
        vals.append(both[64:128])
    dz = jnp.concatenate(parts + vals, axis=0).astype(BF16)
    dzp = nn(r.sprt[...], dz).astype(BF16)
    dh1 = tn(dzp, r.g1[...].reshape(1024, D))
    n1 = r.x_s[...] * inv1
    gsum1 = jnp.sum(dh1 * n1, axis=0, keepdims=True)
    r.gain_s[3] = jnp.broadcast_to(gsum1, (8, D))
    gain_sum = nn((jnp.concatenate([r.gain_s[3]] * 4, axis=0) * r.owner[...]).astype(BF16), r.fold[...])
    r.g1[...] = (nn(dzp, r.h1[...]) + place_row(30, gain_sum)).astype(BF16).reshape(32, 32, D)
    copy1, fold1 = folder(r.g1, r.r1, r.d1fold)
    sum1 = reducer(r.g1, (r.ava, r.avb, r.avp, r.avm, r.aua, r.aub, r.aup, r.aum), r.d1sem, 16)
    for du, dv in order:
        copy1(dv, du).start()
    sum2.end()
    total2 = r.g2[s].astype(F32)
    down2 = jnp.concatenate([total2[128 + 32 * k : 160 + 32 * k, 0:512] for k in range(3)], axis=1)
    for k in range(4):
        r.zs2[k] = total2[0:128, 144 * k : 144 * k + 144].astype(BF16)
        r.zd2[k] = down2[:, 384 * k : 384 * k + 384].astype(BF16)
    z2 = SumZ(b, s, [
        (r.zs2, (r.zs2p, r.zs2m, r.zs2a, r.zs2b)), (r.zd2, (r.zd2p, r.zd2m, r.zd2a, r.zd2b)),
    ], r.z2sem)
    z2.begin()
    g1v = dh1 * r.gain_s[0, 0:1, :]
    tg = r.mix_s[...] + inv1 * (g1v - n1 * (jnp.sum(g1v * n1, axis=-1, keepdims=True) * (1.0 / D)))
    for q in range(2):
        r.tgrad[q] = tg[PIECE * q : PIECE * (q + 1), :].T.astype(BF16)
    homeward(3, r.tgrad, r.tgrad_o, *begin)
    for offset in order:
        fold1(*offset)
        sum1.event(*offset)
        if offset == (0, 3):
            z2.middle()
    sum1.end()
    total1 = r.g1[s].astype(F32)
    for k in range(4):
        r.zs1[k] = total1[:, 144 * k : 144 * k + 144].astype(BF16)
    z1 = SumZ(b, s, [(r.zs1, (r.zs1p, r.zs1m, r.zs1a, r.zs1b))], r.z1sem)
    z1.begin()
    raw2, down_sum = z2.result()
    r.raw_o[32:160, :] = raw2
    r.down_o[...] = down_sum
    z1.middle()
    r.raw_o[0:32, :] = z1.result()[0]
    for offset in order:
        copy2(*offset).wait_send()
        copy1(*offset).wait_send()
    for part in (sumk, sum2, sum1, z2, z1):
        part.finish()
    for k, src, dst in ((2, r.mixed, r.mixed_o), (3, r.tgrad, r.tgrad_o)):
        homeward(k, src, dst, *ended)
        homeward_wait(k, src, dst)


def layer_call(shards, tokens, cot, tables, constants):
    any_ = pl.BlockSpec(memory_space=pl.ANY)
    vm = pl.BlockSpec(memory_space=pltpu.VMEM)
    return pl.pallas_call(
        layer_kernel,
        out_shape=(
            jax.ShapeDtypeStruct((2, D, PIECE), BF16),
            jax.ShapeDtypeStruct((2, D, PIECE), BF16),
            jax.ShapeDtypeStruct((160, 144), F32),
            jax.ShapeDtypeStruct((32, 384), F32),
        ),
        in_specs=[vm] * 8 + [any_] * 2 + [vm] * 5 + [any_] * 3,
        out_specs=(any_, any_, vm, vm),
        scratch_shapes=[pltpu.VMEM(shape, kind) for shape, kind in SCRATCH.values()]
        + [pltpu.SemaphoreType.DMA(shape) for shape in SEMS.values()],
        compiler_params=pltpu.CompilerParams(
            collective_id=0, has_side_effects=True, vmem_limit_bytes=VLIMIT
        ),
        name="decoder_layer",
    )(*shards, tokens, cot, *tables, *constants)


def finish_kernel(mixed, tgrad, raw, down, mixed_o, tgrad_o, g1, wq, wk, wv, wo, g2, wg, wu, wd):
    mixed_o[...] = mixed[...]
    tgrad_o[...] = tgrad[...]
    g1[...] = raw[30:31, 0:18]
    g2[...] = raw[50:51, 0:18]
    for at, ref in ((0, wq), (18, wk), (24, wv), (32, wo), (64, wg), (112, wu)):
        ref[...] = raw[at : at + ref.shape[0], :]
    wd[...] = down[0:18, :]


def finish_call(mixed, tgrad, raw, down):
    vm = pl.BlockSpec(memory_space=pltpu.VMEM)
    shapes = [(1, 18), (18, 144), (6, 144), (6, 144), (18, 144), (1, 18), (48, 144), (48, 144), (18, 384)]
    return pl.pallas_call(
        finish_kernel,
        out_shape=tuple([jax.ShapeDtypeStruct((2, D, PIECE), BF16)] * 2 + [jax.ShapeDtypeStruct(n, F32) for n in shapes]),
        in_specs=[vm] * 4,
        out_specs=(vm,) * 11,
        name="write_outputs",
    )(mixed, tgrad, raw, down)


def body(
    tokens, doc_lengths, first_gain, query_weight, key_matrix, value_matrix,
    output_weight, second_gain, gate_weight, up_weight, down_weight, cotangent,
):
    s = lax.axis_index("seq")
    c, p = s % 2, s // 2
    gains = jnp.stack([first_gain, second_gain])
    spread = jnp.asarray(spread_matrix())
    sprt = jnp.asarray(spread_matrix().T.copy())
    fold, owner = (jnp.asarray(m) for m in gain_matrix())

    lens = lax.dynamic_index_in_dim(doc_lengths[:, 0, :], c, 0, False)
    starts = [jnp.zeros((), jnp.int32), lens[0], lens[0] + lens[1]]
    at = jnp.arange(PIECE, dtype=jnp.int32)
    spots = jnp.stack([p * PIECE + at, (31 - p) * PIECE + at])
    begins = jnp.where(spots >= starts[2], starts[2], jnp.where(spots >= starts[1], starts[1], 0))
    rates = THETA ** (-2.0 * jnp.arange(HD // 2, dtype=F32) / HD)
    angles = (spots - begins).reshape(T).astype(F32)[None, :] * rates[:, None]
    cos, sin = jnp.cos(angles), jnp.sin(angles)
    qpos = jnp.broadcast_to(spots[:, None], (2, 3, PIECE)).reshape(1, LANES)
    qstart = jnp.broadcast_to(begins[:, None], (2, 3, PIECE)).reshape(1, LANES)

    shards = [
        query_weight.T, key_matrix.T, value_matrix.T, output_weight.T,
        gate_weight.T, up_weight.T, down_weight.T, gains,
    ]
    turn = lambda a: jnp.swapaxes(a[:, 0], 1, 2)
    mixed, tgrad, raw, down = layer_call(
        shards, turn(tokens), turn(cotangent), (cos, sin, qpos, qstart, owner), (spread, sprt, fold)
    )
    mixed, tgrad, g1, wq, wk, wv, wo, g2, wg, wu, wd = finish_call(mixed, tgrad, raw, down)
    back = lambda a: jnp.swapaxes(a, 1, 2)[:, None]
    return (
        back(mixed), back(tgrad), g1.reshape(18), wq.T, wk.T, wv.T, wo.T, g2.reshape(18), wg.T, wu.T, wd.T,
    )


def solution(mesh):
    weight = P("batch", "seq")
    rows = P(None, "batch", "seq", None)
    return jax.shard_map(
        body,
        mesh=mesh,
        in_specs=(
            rows, P(None, "batch", None), P("seq"), weight, weight, weight, weight,
            P("seq"), weight, weight, weight, rows,
        ),
        out_specs=(
            rows, rows, P("seq"), weight, weight, weight, weight,
            P("seq"), weight, weight, weight,
        ),
        check_vma=False,
    )
```

time: 1410 us -> 173 us (0.12)
  waiting for transfers between devices: 753 us -> 0 us
  blocking collectives: 399 us -> 0 us
  Pallas kernels: 0 us -> 163 us
  local copies, waits for them, and re-layouts: 116 us -> 2.43 us
  matrix products: 62.4 us -> 0 us
  starting transfers between devices: 22.1 us -> 0 us
  between operations: 19 us -> 2.16 us
  other arithmetic: 20 us -> 3.34 us
    unnamed x41 -> x0, waiting for transfers between devices: 525 us -> none
    unnamed x3 -> x0, blocking collectives: 207 us -> none
    all_gather x11 -> x0, blocking collectives: 180 us -> none  [the longest x1 25.1 us: fetch(): lax.all_gather(tall[1], 'seq', axis=1, tiled=True)]
    pallas_call x0 -> x2, Pallas kernels: none -> 163 us  [the longest x1 161 us: layer_call(): pl.pallas_call(layer_kernel, out_shape=(jax.ShapeDtypeStruct((2, D, PIECE...]
    all_gather x7 -> x0, waiting for transfers between devices: 140 us -> none  [the longest x1 42.4 us: fetch(): lax.all_gather(tall[6], 'seq', axis=1, tiled=True)]
    unnamed x221 -> x2, local copies, waits for them, and re-layouts: 105 us -> 0.65 us
    reduce_scatter x2 -> x0, waiting for transfers between devices: 89.1 us -> none  [the longest x1 78.1 us: body(): lax.psum_scatter(totals[5].astype(jnp.bfloat16), 'seq', scatter_dimension...]
    dot_general x56 -> x0, matrix products: 62.4 us -> none  [the longest x4 5.84 us: block_scores(): jnp.einsum('sqcgd,skcd->scgqk', query_rows_local, key_rows, preferred_ele...]
  transfers between devices with their start and end apart: 29 -> 0, of which waited for: 19 -> 0; matrix products, arithmetic and copies ran while one was open for 11% -> 0% of each run, Pallas kernels for 0% -> 0%
where the time goes in v2:
time: 173 us; the launch traced here: 171 us
  Pallas kernels  163 us (94%)
  other arithmetic  3.34 us (2%)
  local copies, waits for them, and re-layouts  2.43 us (1%)
  between operations  2.16 us (1%)
    pallas_call x1, Pallas kernels, layer_call(): pl.pallas_call(layer_kernel, out_shape=(jax.ShapeDtypeStruct((2, D, PIECE...  161 us

profile of v2, /device:TPU:0, one launch (start us, length us, event | category | flops | bytes accessed | tf_op | source)
XLA Modules:
  0.0 171.1 jit_solution(8349236993217107143)
XLA Ops:
  0.6 0.0 copy-start
  0.7 0.6 copy-done
  1.3 1.2 pad_maximum_fusion.refs_7_
  2.5 0.6 fusion.2
  4.4 0.7 fusion.1
  5.1 0.7 compare_select_fusion.1
  5.8 0.6 reshape.103.refs_13_
  6.4 0.6 reshape.102.refs_12_
  6.9 0.8 multiply_sine_fusion
  7.8 161.1 %decoder_layer.1 = (bf16[2,576,128]{2,1,0:T(8,128)(2,1)}, bf16[2,576,128]{2,1,0:T(8,128)(2,1)}, f32[160,144]{1,0:T(8,128)}, f32[32,384]{1,0:T(8,128)}) custom-call(bf16[18,144]{1,0:T(8,128)(2,1)} %bitcast.43, bf16[6,144]{1,0:T(8,128)(2,1)} %bitcast.45, bf16[6,144]{1,0:T(8,128)(2,1)} %bitcast.46, bf16[18,144]{1,0:T(8,128)(2,1)} %bitcast.44, ...), custom_call_target="tpu_custom_call" | custom-call | tf_op jit(solution)/shard_map/decoder_layer/pallas_call | solution.py:904
  168.9 2.0 %write_outputs.1 = (bf16[2,576,128]{2,1,0:T(8,128)(2,1)}, bf16[2,576,128]{2,1,0:T(8,128)(2,1)}, f32[1,18]{1,0:T(1,128)}, f32[18,144]{1,0:T(8,128)}, f32[6,144]{1...) custom-call(bf16[2,576,128]{2,1,0:T(8,128)(2,1)} %get-tuple-element., ...), custom_call_target="tpu_custom_call" | custom-call | tf_op jit(solution)/shard_map/write_outputs/pallas_call | solution.py:936
  (5 shorter events, 0.0 us)
Async XLA Ops:
  0.6 0.7 copy-start

commit v3 on v2

--- a/solution.py
+++ b/solution.py
@@ -69,6 +69,16 @@
     return b, s, c, p, lax.div(p, 4), lax.rem(p, 4)
 
 
+def chip_of(piece):
+    i = jnp.minimum(piece, 31 - piece)
+    half = lax.div(i, 2)
+    return jnp.where(lax.rem(i, 2) == 0, half, 15 - half)
+
+
+def early_piece(chip):
+    return jnp.where(chip < 8, 2 * chip, 31 - 2 * chip)
+
+
 def seq_of(y, x, c):
     return (y * 4 + x) * 2 + c
 
@@ -86,7 +96,7 @@
 
 def neighbours(b, s, c, y, x):
     found = [(b, seq_of(y, x, 1 - c))]
-    for d in (1, 3):
+    for d in (1, 2, 3):
         found += [
             (hop(b, d), s),
             (b, seq_of(y, hop(x, d), c)),
@@ -96,10 +106,12 @@
 
 
 class Ring:
-    def __init__(self, dev, ss, rs):
-        self.dev, self.ss, self.rs = dev, ss, rs
+    def __init__(self, dev, ss, rs, direct=False):
+        self.dev, self.ss, self.rs, self.direct = dev, ss, rs, direct
 
     def copy(self, n, src, dst):
+        if n == 2 and self.direct:
+            return rcopy(src, dst, self.ss.at[n], self.rs.at[n], self.dev(2, 0))
         du, dv = {0: (1, 0), 1: (3, 0), 2: (1, 0), 3: (3, 0)}.get(n, (0, 1 if n // 4 in (1, 3) else 3))
         return rcopy(src, dst, self.ss.at[n], self.rs.at[n], self.dev(du, dv))
 
@@ -166,8 +178,8 @@
 
 
 class Gather:
-    def __init__(self, plane, view, own, sems, swap=None):
-        self.ring = Ring(plane.dev, sems.at[0], sems.at[1])
+    def __init__(self, plane, view, own, sems, swap=None, direct=False):
+        self.ring = Ring(plane.dev, sems.at[0], sems.at[1], direct)
         self.view, self.own, self.swap = view, own, swap
         self.later = []
 
@@ -190,6 +202,8 @@
     def begin_u(self):
         self.send(0, 0, 0)
         self.send(1, 0, 0)
+        if self.ring.direct:
+            self.send(2, 0, 0)
 
     def begin_v(self):
         self.send(4, 0, 0)
@@ -199,14 +213,18 @@
     def near(self):
         for n, du in ((0, 3), (1, 1)):
             self.arrive(n, du, 0)
-            self.send(2 + n, du, 0, n)
+            if not self.ring.direct:
+                self.send(2 + n, du, 0, n)
             self.send(4 + du, du, 0)
             self.send(8 + du, du, 0)
             self.done(du, 0)
 
     def far(self):
-        self.arrive(2, 2, 0, 0)
-        self.arrive(3, 2, 0, 1)
+        if self.ring.direct:
+            self.arrive(2, 2, 0)
+        else:
+            self.arrive(2, 2, 0, 0)
+            self.arrive(3, 2, 0, 1)
         self.send(6, 2, 0)
         self.send(10, 2, 0)
         self.done(2, 0)
@@ -234,13 +252,16 @@
 
 
 class Reduce:
-    def __init__(self, plane, view, add, bufs, sems):
-        self.ring = Ring(plane.dev, sems.at[0], sems.at[1])
+    def __init__(self, plane, view, add, bufs, sems, direct=False):
+        self.ring = Ring(plane.dev, sems.at[0], sems.at[1], direct)
         self.view, self.add = view, add
         va, vb, vp, vm, ua, ub, up, um = bufs
         self.pieces = {
             2: (2, 0, 0, ua), 3: (2, 0, 1, ub), 0: (1, 0, None, up), 1: (3, 0, None, um),
         }
+        if direct:
+            self.pieces[2] = (2, 0, None, ua)
+            del self.pieces[3]
         for w in range(4):
             self.pieces[12 + w] = (w, 2, 0, va.at[w])
             self.pieces[16 + w] = (w, 2, 1, vb.at[w])
@@ -268,7 +289,10 @@
         else:
             self.take(4 + du, du, 0)
             self.take(8 + du, du, 0)
-            if du == 2:
+            if self.ring.direct:
+                if du:
+                    self.copy({1: 0, 2: 2, 3: 1}[du]).start()
+            elif du == 2:
                 self.copy(2).start()
                 self.copy(3).start()
             elif du == 1:
@@ -281,6 +305,8 @@
     def end(self):
         self.take(0, 0, 0)
         self.take(1, 0, 0)
+        if self.ring.direct:
+            self.take(2, 0, 0)
 
     def finish(self):
         for n in self.pieces:
@@ -342,7 +368,7 @@
     "blk1": ((32, D), BF16), "blk2": ((ROWS, D), BF16),
     "g1": ((32, 32, D), BF16), "g2": ((32, ROWS, D), BF16),
     "tok": ((2, D, PIECE), BF16), "cot": ((2, D, PIECE), BF16),
-    "gain_s": ((4, 8, D), F32), "x_s": ((T, D), F32), "h1": ((T, D), BF16),
+    "qpos": ((1, LANES), jnp.int32), "qstart": ((1, LANES), jnp.int32), "gain_s": ((4, 8, D), F32), "x_s": ((T, D), F32), "h1": ((T, D), BF16),
     "kv": ((KV, T, 128), BF16), "qt": ((KV, 128, LANES), BF16), "dot": ((KV, 128, LANES), BF16),
     "kva": ((16, KV, T, 128), BF16),
     "m_s": ((KV, 1, LANES), F32), "l_s": ((KV, 1, LANES), F32), "delta": ((KV, 1, LANES), F32),
@@ -363,21 +389,21 @@
     "r1": ((16, 32, D), BF16),
     "ava": ((4, 16, D), BF16), "avb": ((4, 16, D), BF16),
     "avp": ((4, 32, D), BF16), "avm": ((4, 32, D), BF16),
-    "aua": ((16, D), BF16), "aub": ((16, D), BF16),
+    "aua": ((32, D), BF16), "aub": ((16, D), BF16),
     "aup": ((32, D), BF16), "aum": ((32, D), BF16),
     "zs2": ((4, 128, 144), BF16), "zd2": ((4, 32, 384), BF16), "zs1": ((4, 32, 144), BF16),
     "zs2p": ((128, 144), BF16), "zs2m": ((128, 144), BF16), "zs2a": ((64, 144), BF16), "zs2b": ((64, 144), BF16),
     "zd2p": ((32, 384), BF16), "zd2m": ((32, 384), BF16), "zd2a": ((16, 384), BF16), "zd2b": ((16, 384), BF16),
-    "zs1p": ((32, 144), BF16), "zs1m": ((32, 144), BF16), "zs1a": ((16, 144), BF16), "zs1b": ((16, 144), BF16),
+    "zs1l": ((3, 32, 144), BF16),
 }
 SEMS = {
     "lsem": (4,), "zsem": (2, 2, 4), "zz": (4, 2, 2), "zl": (4,),
     "g1sem": (2, 20), "g1swap": (2, 16), "g2sem": (2, 20), "g2swap": (2, 16), "kvsem": (2, 20),
     "dksem": (2, 20), "d2fold": (2, 16), "d2sem": (2, 20), "d1fold": (2, 16), "d1sem": (2, 20),
-    "z2sem": (2, 2, 4), "z1sem": (2, 1, 4),
+    "z2sem": (2, 2, 4), "z1sem": (2, 4), "zasem": (2, 4),
 }
 INPUTS = (
-    "wq", "wk", "wv", "wo", "wg", "wu", "wd", "gains", "tokens", "cotin", "cos", "sin", "qpos", "qstart",
+    "wq", "wk", "wv", "wo", "wg", "wu", "wd", "gains", "tokens", "cotin", "cos", "sin", "begins",
     "owner", "spread_in", "sprt_in", "fold_in",
 )
 OUTPUTS = ("mixed_o", "tgrad_o", "raw_o", "down_o")
@@ -393,10 +419,11 @@
     r = Refs(refs)
     plane = Plane()
     b, s, c, p, y, x = plane.b, plane.s, plane.c, plane.p, plane.y, plane.x
-    early = jnp.minimum(s, 31 - s)
+    target = 2 * chip_of(s)
     slot = lax.div(s, 16)
+    e = early_piece(p)
     bar = hail(neighbours(b, s, c, y, x))
-    around = [2 * early, 2 * early + 1, p, 31 - p]
+    around = [target, target + 1, e, 31 - e]
     for peer in around:
         @pl.when(peer != s)
         def _():
@@ -407,6 +434,11 @@
     ]
     for cp in constants:
         cp.start()
+    for lane in range(0, LANES, PIECE):
+        q = lane // 384
+        at = (31 - e if q else e) * PIECE
+        r.qpos[:, lane : lane + PIECE] = at + lax.broadcasted_iota(jnp.int32, (1, PIECE), 1)
+        r.qstart[:, lane : lane + PIECE] = r.begins[q : q + 1, :]
     r.raw_f[...] = jnp.zeros_like(r.raw_f)
     r.dwn_f[...] = jnp.zeros_like(r.dwn_f)
     for at, ref in ((0, r.wq), (18, r.wk), (24, r.wv), (32, r.wo), (64, r.wg), (112, r.wu)):
@@ -415,7 +447,7 @@
     r.dwn_f[0:18, :] = r.wd[...].astype(F32)
     r.za[pl.ds(b, 1)] = r.raw_f[...].astype(BF16)[None]
     r.zd[pl.ds(b, 1)] = r.dwn_f[...].astype(BF16)[None]
-    peers = 7
+    peers = 10
     for peer in around:
         peers = peers + jnp.where(peer != s, 1, 0)
     pl.semaphore_wait(bar, peers)
@@ -423,8 +455,8 @@
     def zcopies(n, at, part):
         dev = (hop(b, 1 if n in (0, 2) else 3), s)
         found = []
-        for k, (ref, rows) in enumerate(((r.za, 80), (r.zd, 16))):
-            view = ref.at[at] if part is None else ref.at[at, pl.ds(rows * part, rows)]
+        for k, (ref, low, rows) in enumerate(((r.za, 32, 64), (r.zd, 0, 16))):
+            view = ref.at[at, pl.ds(low, 2 * rows) if part is None else pl.ds(low + rows * part, rows)]
             found.append(rcopy(view, view, r.zsem.at[0, k, n], r.zsem.at[1, k, n], dev))
         return found
 
@@ -432,12 +464,17 @@
         for cp in copies:
             cp.start()
 
+    def acopy(d, at):
+        view = r.za.at[at, pl.ds(0, 32)]
+        return rcopy(view, view, r.zasem.at[0, d], r.zasem.at[1, d], (hop(b, d), s))
+
+    start([acopy(d, b) for d in (1, 2, 3)])
     zsent = [zcopies(0, b, None), zcopies(1, b, None)]
     start(zsent[0] + zsent[1])
 
     def outward(k, src_ref, dst_ref, act_remote, act_local):
         for m in (0, 1):
-            dst = 2 * early + m
+            dst = target + m
 
             @pl.when(dst != s)
             def _():
@@ -448,13 +485,13 @@
                 act_local(pltpu.make_async_copy(src_ref.at[m], dst_ref.at[slot], r.zl.at[k]))
 
     def outward_wait(k, src_ref, dst_ref):
-        for q, src in enumerate((p, 31 - p)):
+        for q, src in enumerate((e, 31 - e)):
             @pl.when(src != s)
             def _():
                 rcopy(src_ref.at[0], dst_ref.at[q], r.zz.at[k, 0, 0], r.zz.at[k, 1, q], (b, src)).wait_recv()
 
     def homeward(k, src_ref, dst_ref, act_remote, act_local):
-        for q, dst in enumerate((p, 31 - p)):
+        for q, dst in enumerate((e, 31 - e)):
             @pl.when(dst != s)
             def _():
                 act_remote(rcopy(src_ref.at[q], dst_ref.at[c], r.zz.at[k, 0, q], r.zz.at[k, 1, c], (b, dst)))
@@ -465,7 +502,7 @@
 
     def homeward_wait(k, src_ref, dst_ref):
         for m in (0, 1):
-            src = 2 * early + m
+            src = target + m
 
             @pl.when(src != s)
             def _():
@@ -474,47 +511,47 @@
     begin = (lambda cp: cp.start(), lambda cp: cp.start())
     ended = (lambda cp: cp.wait_send(), lambda cp: cp.wait())
     outward(0, r.tokens, r.tok, *begin)
-    outward(1, r.cotin, r.cot, *begin)
-
+
+    for d in (1, 2, 3):
+        acopy(d, hop(b, 4 - d)).wait_recv()
+    r.blk1[...] = jnp.concatenate([r.za[i, 0:32, :].astype(F32) for i in range(4)], axis=1).astype(BF16)
+
+    def weights(ref, own, sems, swap_sems, half, direct=False):
+        def view(du, dv, part=None):
+            at = 2 * plane.index(du, dv) + c
+            return ref.at[at] if part is None else ref.at[at, pl.ds(half * part, half)]
+
+        def swap(du, dv):
+            n = plane.common(du, dv)
+            dst = view(du, dv)
+            src = own if (du, dv) == (0, 0) else dst
+            return rcopy(src, dst, swap_sems.at[0, n], swap_sems.at[1, n], plane.other)
+
+        return Gather(plane, view, own, sems, swap, direct)
+
+    first = weights(r.g1, r.blk1, r.g1sem, r.g1swap, 16, True)
+    second = weights(r.g2, r.blk2, r.g2sem, r.g2swap, ROWS // 2)
+    first.begin_u()
+    first.begin_v()
+    r.g1[pl.ds(s, 1)] = r.blk1[...][None]
     for n, way in ((0, 3), (1, 1)):
         for cp in zcopies(n, hop(b, way), None):
             cp.wait_recv()
         zsent.append(zcopies(2 + n, hop(b, way), n))
         start(zsent[-1])
+    first.near()
+    first.line(0)
+    first.far()
     for n in (2, 3):
         for cp in zcopies(n, hop(b, 2), n - 2):
             cp.wait_recv()
-    main = jnp.concatenate([r.za[i].astype(F32) for i in range(4)], axis=1).astype(BF16)
-    r.blk1[...] = main[0:32]
-
-    def weights(ref, own, sems, swap_sems, half):
-        def view(du, dv, part=None):
-            at = 2 * plane.index(du, dv) + c
-            return ref.at[at] if part is None else ref.at[at, pl.ds(half * part, half)]
-
-        def swap(du, dv):
-            n = plane.common(du, dv)
-            dst = view(du, dv)
-            src = own if (du, dv) == (0, 0) else dst
-            return rcopy(src, dst, swap_sems.at[0, n], swap_sems.at[1, n], plane.other)
-
-        return Gather(plane, view, own, sems, swap)
-
-    first = weights(r.g1, r.blk1, r.g1sem, r.g1swap, 16)
-    second = weights(r.g2, r.blk2, r.g2sem, r.g2swap, ROWS // 2)
-    first.begin_u()
-    first.begin_v()
-    r.g1[pl.ds(s, 1)] = r.blk1[...][None]
     down = jnp.concatenate([r.zd[i] for i in range(4)], axis=1)
-    r.blk2[0:128, :] = main[32:160]
+    r.blk2[0:128, :] = jnp.concatenate([r.za[i, 32:160, :].astype(F32) for i in range(4)], axis=1).astype(BF16)
     r.blk2[128:224, 512:576] = jnp.zeros((96, 64), BF16)
     for k in range(3):
         r.blk2[128 + 32 * k : 160 + 32 * k, 0:512] = down[:, 512 * k : 512 * (k + 1)]
-    first.near()
     second.begin_u()
     r.g2[pl.ds(s, 1)] = r.blk2[...][None]
-    first.line(0)
-    first.far()
     outward_wait(0, r.tokens, r.tok)
     outward(0, r.tokens, r.tok, *ended)
     r.x_s[...] = token_rows(r.tok)
@@ -523,6 +560,7 @@
     second.begin_v()
     for w in (0, 3, 1, 2):
         first.last(w)
+    second.near()
     first.finish()
     for cp in constants:
         cp.wait()
@@ -562,6 +600,7 @@
     keys = Gather(plane, kview(r.kva), r.kv, r.kvsem)
     keys.begin_u()
     keys.begin_v()
+    outward(1, r.cotin, r.cot, *begin)
     r.kva[pl.ds(p, 1)] = r.kv[...][None]
     for h in range(HEADS):
         q = (rot(z[64 * h : 64 * h + 64]).astype(BF16).astype(F32) * 0.125).astype(BF16)
@@ -598,17 +637,16 @@
         r.acc[h, :, lanes] = r.acc[h, :, lanes] * a + tn(block, pt.astype(BF16))[64:128]
 
     def allowed():
-        return diagonal_mask(p, r.qpos[...], r.qstart[...])
+        return diagonal_mask(e, r.qpos[...], r.qstart[...])
 
     mask = allowed()
     for h in range(KV):
         step(r.kv[h], h, every, mask, None)
 
     events = {
-        1: [keys.near, second.near], 2: [lambda: keys.line(0)], 3: [keys.far, lambda: second.line(0)],
-        4: [lambda: keys.line(3)], 5: [lambda: keys.line(1), second.far], 7: [lambda: keys.line(2)],
-        8: [lambda: second.line(3)], 10: [lambda: second.line(1)],
-        12: [lambda: keys.last(0), lambda: second.line(2)], 13: [lambda: keys.last(3)],
+        1: [keys.near, lambda: second.line(0)], 2: [lambda: keys.line(0)], 3: [keys.far, second.far],
+        4: [lambda: keys.line(3)], 5: [lambda: keys.line(1)], 6: [lambda: second.line(3)], 7: [lambda: keys.line(2)],
+        8: [lambda: second.line(1)], 10: [lambda: second.line(2)], 12: [lambda: keys.last(0)], 13: [lambda: keys.last(3)],
         14: [lambda: keys.last(1), lambda: second.last(0)], 15: [lambda: keys.last(2)],
     }
 
@@ -620,19 +658,20 @@
                     event()
 
         j = plane.index(pick(i, [o[0] for o in FORWARD]), pick(i, [o[1] for o in FORWARD]))
-
-        @pl.when((j < p) & (j > 0))
+        ej = early_piece(j)
+
+        @pl.when((ej < e) & (j > 0))
         def _():
             for h in range(KV):
                 step(r.kva[j, h, 0:PIECE, :], h, every, None, None)
 
-        @pl.when((j < p) & (j == 0))
+        @pl.when((ej < e) & (j == 0))
         def _():
             keep = first_mask(r.qstart[...])
             for h in range(KV):
                 step(r.kva[0, h, 0:PIECE, :], h, every, keep, None)
 
-        @pl.when(j > p)
+        @pl.when(ej > e)
         def _():
             drop = r.qstart[:, late] >= PIECE
             for h in range(KV):
@@ -662,7 +701,7 @@
         second.last(w)
     keys.finish()
     second.finish()
-    for group in zsent:
+    for group in zsent + [[acopy(d, b) for d in (1, 2, 3)]]:
         for cp in group:
             cp.wait_send()
 
@@ -733,7 +772,7 @@
 
         return copy, fold_in
 
-    def reducer(ref, bufs, sems, half):
+    def reducer(ref, bufs, sems, half, direct=False):
         def view(du, dv, part=None):
             at = 2 * plane.index(du, dv) + c
             return ref.at[at] if part is None else ref.at[at, pl.ds(half * part, half)]
@@ -743,7 +782,7 @@
             where = (at,) if part is None else (at, pl.ds(half * part, half))
             ref[where] = ref[where] + buf[...]
 
-        return Reduce(plane, view, add, bufs, sems)
+        return Reduce(plane, view, add, bufs, sems, direct)
 
     copy2, fold2 = folder(r.g2, r.r2, r.d2fold)
     sum2 = reducer(r.g2, (r.wva, r.wvb, r.wvp, r.wvm, r.wua, r.wub, r.wup, r.wum), r.d2sem, ROWS // 2)
@@ -792,23 +831,24 @@
 
     def visit_back(i, carry):
         j = plane.index(pick(i, [o[0] for o in BACKWARD]), pick(i, [o[1] for o in BACKWARD]))
-
-        @pl.when(j < p)
+        ej = early_piece(j)
+
+        @pl.when(ej < e)
         def _():
             r.sent[j, :, PIECE:T, :] = jnp.zeros((KV, PIECE, 128), BF16)
 
-        @pl.when((j < p) & (j > 0))
+        @pl.when((ej < e) & (j > 0))
         def _():
             for h in range(KV):
                 r.sent[j, h, 0:PIECE, :] = back(r.kva[j, h, 0:PIECE, :], h, every, None, None).astype(BF16)
 
-        @pl.when((j < p) & (j == 0))
+        @pl.when((ej < e) & (j == 0))
         def _():
             keep = first_mask(r.qstart[...])
             for h in range(KV):
                 r.sent[0, h, 0:PIECE, :] = back(r.kva[0, h, 0:PIECE, :], h, every, keep, None).astype(BF16)
 
-        @pl.when(j > p)
+        @pl.when(ej > e)
         def _():
             drop = r.qstart[:, late] >= PIECE
             for h in range(KV):
@@ -854,7 +894,7 @@
     gain_sum = nn((jnp.concatenate([r.gain_s[3]] * 4, axis=0) * r.owner[...]).astype(BF16), r.fold[...])
     r.g1[...] = (nn(dzp, r.h1[...]) + place_row(30, gain_sum)).astype(BF16).reshape(32, 32, D)
     copy1, fold1 = folder(r.g1, r.r1, r.d1fold)
-    sum1 = reducer(r.g1, (r.ava, r.avb, r.avp, r.avm, r.aua, r.aub, r.aup, r.aum), r.d1sem, 16)
+    sum1 = reducer(r.g1, (r.ava, r.avb, r.avp, r.avm, r.aua, r.aub, r.aup, r.aum), r.d1sem, 16, True)
     for du, dv in order:
         copy1(dv, du).start()
     sum2.end()
@@ -881,18 +921,26 @@
     total1 = r.g1[s].astype(F32)
     for k in range(4):
         r.zs1[k] = total1[:, 144 * k : 144 * k + 144].astype(BF16)
-    z1 = SumZ(b, s, [(r.zs1, (r.zs1p, r.zs1m, r.zs1a, r.zs1b))], r.z1sem)
-    z1.begin()
+    z1 = [
+        rcopy(r.zs1.at[hop(b, d)], r.zs1l.at[d - 1], r.z1sem.at[0, d], r.z1sem.at[1, d], (hop(b, d), s))
+        for d in (1, 2, 3)
+    ]
+    start(z1)
     raw2, down_sum = z2.result()
     r.raw_o[32:160, :] = raw2
     r.down_o[...] = down_sum
-    z1.middle()
-    r.raw_o[0:32, :] = z1.result()[0]
+    total = r.zs1[b].astype(F32)
+    for d, cp in enumerate(z1):
+        cp.wait_recv()
+        total += r.zs1l[d].astype(F32)
+    r.raw_o[0:32, :] = total
     for offset in order:
         copy2(*offset).wait_send()
         copy1(*offset).wait_send()
-    for part in (sumk, sum2, sum1, z2, z1):
+    for part in (sumk, sum2, sum1, z2):
         part.finish()
+    for cp in z1:
+        cp.wait_send()
     for k, src, dst in ((2, r.mixed, r.mixed_o), (3, r.tgrad, r.tgrad_o)):
         homeward(k, src, dst, *ended)
         homeward_wait(k, src, dst)
@@ -909,7 +957,7 @@
             jax.ShapeDtypeStruct((160, 144), F32),
             jax.ShapeDtypeStruct((32, 384), F32),
         ),
-        in_specs=[vm] * 8 + [any_] * 2 + [vm] * 5 + [any_] * 3,
+        in_specs=[vm] * 8 + [any_] * 2 + [vm] * 4 + [any_] * 3,
         out_specs=(any_, any_, vm, vm),
         scratch_shapes=[pltpu.VMEM(shape, kind) for shape, kind in SCRATCH.values()]
         + [pltpu.SemaphoreType.DMA(shape) for shape in SEMS.values()],
@@ -956,21 +1004,19 @@
     lens = lax.dynamic_index_in_dim(doc_lengths[:, 0, :], c, 0, False)
     starts = [jnp.zeros((), jnp.int32), lens[0], lens[0] + lens[1]]
     at = jnp.arange(PIECE, dtype=jnp.int32)
-    spots = jnp.stack([p * PIECE + at, (31 - p) * PIECE + at])
+    e = early_piece(p)
+    spots = jnp.stack([e * PIECE + at, (31 - e) * PIECE + at])
     begins = jnp.where(spots >= starts[2], starts[2], jnp.where(spots >= starts[1], starts[1], 0))
     rates = THETA ** (-2.0 * jnp.arange(HD // 2, dtype=F32) / HD)
     angles = (spots - begins).reshape(T).astype(F32)[None, :] * rates[:, None]
     cos, sin = jnp.cos(angles), jnp.sin(angles)
-    qpos = jnp.broadcast_to(spots[:, None], (2, 3, PIECE)).reshape(1, LANES)
-    qstart = jnp.broadcast_to(begins[:, None], (2, 3, PIECE)).reshape(1, LANES)
-
     shards = [
         query_weight.T, key_matrix.T, value_matrix.T, output_weight.T,
         gate_weight.T, up_weight.T, down_weight.T, gains,
     ]
     turn = lambda a: jnp.swapaxes(a[:, 0], 1, 2)
     mixed, tgrad, raw, down = layer_call(
-        shards, turn(tokens), turn(cotangent), (cos, sin, qpos, qstart, owner), (spread, sprt, fold)
+        shards, turn(tokens), turn(cotangent), (cos, sin, begins, owner), (spread, sprt, fold)
     )
     mixed, tgrad, g1, wq, wk, wv, wo, g2, wg, wu, wd = finish_call(mixed, tgrad, raw, down)
     back = lambda a: jnp.swapaxes(a, 1, 2)[:, None]

time: 173 us -> 159 us (0.919)
  Pallas kernels: 163 us -> 150 us
    pallas_call x1, Pallas kernels: 161 us -> 148 us  [layer_call(): pl.pallas_call(layer_kernel, out_shape=(jax.ShapeDtypeStruct((2, D, PIECE...]
where the time goes in v3:
time: 159 us; the launch traced here: 158 us
  Pallas kernels  150 us (94%)
  other arithmetic  3.9 us (2%)
  between operations  2.15 us (1%)
    pallas_call x1, Pallas kernels, layer_call(): pl.pallas_call(layer_kernel, out_shape=(jax.ShapeDtypeStruct((2, D, PIECE...  148 us

profile of v3, /device:TPU:0, one launch (start us, length us, event | category | flops | bytes accessed | tf_op | source)
XLA Modules:
  0.0 157.5 jit_solution(6285690653339963849)
XLA Ops:
  0.6 0.0 copy-start
  0.7 0.6 copy-done
  1.3 1.2 pad_maximum_fusion.refs_7_
  2.5 0.6 fusion.2
  4.4 1.2 compare_select_fusion.1.refs_12_
  5.6 0.7 fusion.1
  6.3 0.8 multiply_sine_fusion
  7.1 148.2 %decoder_layer.1 = (bf16[2,576,128]{2,1,0:T(8,128)(2,1)}, bf16[2,576,128]{2,1,0:T(8,128)(2,1)}, f32[160,144]{1,0:T(8,128)}, f32[32,384]{1,0:T(8,128)}) custom-call(bf16[18,144]{1,0:T(8,128)(2,1)} %bitcast.43, bf16[6,144]{1,0:T(8,128)(2,1)} %bitcast.45, bf16[6,144]{1,0:T(8,128)(2,1)} %bitcast.46, bf16[18,144]{1,0:T(8,128)(2,1)} %bitcast.44, ...), custom_call_target="tpu_custom_call" | custom-call | tf_op jit(solution)/shard_map/decoder_layer/pallas_call | solution.py:952
  155.4 2.0 %write_outputs.1 = (bf16[2,576,128]{2,1,0:T(8,128)(2,1)}, bf16[2,576,128]{2,1,0:T(8,128)(2,1)}, f32[1,18]{1,0:T(1,128)}, f32[18,144]{1,0:T(8,128)}, f32[6,144]{1...) custom-call(bf16[2,576,128]{2,1,0:T(8,128)(2,1)} %get-tuple-element., ...), custom_call_target="tpu_custom_call" | custom-call | tf_op jit(solution)/shard_map/write_outputs/pallas_call | solution.py:984
  (3 shorter events, 0.0 us)
Async XLA Ops:
  0.6 0.7 copy-start

commit v4 on v3

--- a/solution.py
+++ b/solution.py
@@ -859,11 +859,16 @@
                 @pl.when(i == k)
                 def _():
                     sumk.event(*offset)
-                    fold2(*offset)
-                    sum2.event(*offset)
+                    if offset[1] != 2:
+                        fold2(*offset)
+                        sum2.event(*offset)
 
         return carry
 
+    for offset in BACKWARD:
+        if offset[1] == 2:
+            fold2(*offset)
+            sum2.event(*offset)
     lax.fori_loop(1, 16, visit_back, 0)
     mask = allowed()
     for h in range(KV):

time: 159 us -> 158 us (level)
  no operation moved by 1% of the time
where the time goes in v4:
time: 158 us
  Pallas kernels  151 us (96%)
  other arithmetic  3.9 us (2%)
  between operations  2.15 us (1%)
    pallas_call x1, Pallas kernels, layer_call(): pl.pallas_call(layer_kernel, out_shape=(jax.ShapeDtypeStruct((2, D, PIECE...  149 us

profile of v4, /device:TPU:0, one launch (start us, length us, event | category | flops | bytes accessed | tf_op | source)
XLA Modules:
  0.0 157.9 jit_solution(13555657887890331762)
XLA Ops:
  0.6 0.0 copy-start
  0.7 0.6 copy-done
  1.3 1.2 pad_maximum_fusion.refs_7_
  2.5 0.6 fusion.2
  4.4 1.2 compare_select_fusion.1.refs_12_
  5.6 0.7 fusion.1
  6.3 0.8 multiply_sine_fusion
  7.1 148.6 %decoder_layer.1 = (bf16[2,576,128]{2,1,0:T(8,128)(2,1)}, bf16[2,576,128]{2,1,0:T(8,128)(2,1)}, f32[160,144]{1,0:T(8,128)}, f32[32,384]{1,0:T(8,128)}) custom-call(bf16[18,144]{1,0:T(8,128)(2,1)} %bitcast.43, bf16[6,144]{1,0:T(8,128)(2,1)} %bitcast.45, bf16[6,144]{1,0:T(8,128)(2,1)} %bitcast.46, bf16[18,144]{1,0:T(8,128)(2,1)} %bitcast.44, ...), custom_call_target="tpu_custom_call" | custom-call | tf_op jit(solution)/shard_map/decoder_layer/pallas_call | solution.py:957
  155.7 2.0 %write_outputs.1 = (bf16[2,576,128]{2,1,0:T(8,128)(2,1)}, bf16[2,576,128]{2,1,0:T(8,128)(2,1)}, f32[1,18]{1,0:T(1,128)}, f32[18,144]{1,0:T(8,128)}, f32[6,144]{1...) custom-call(bf16[2,576,128]{2,1,0:T(8,128)(2,1)} %get-tuple-element., ...), custom_call_target="tpu_custom_call" | custom-call | tf_op jit(solution)/shard_map/write_outputs/pallas_call | solution.py:989
  (3 shorter events, 0.0 us)
Async XLA Ops:
  0.6 0.7 copy-start
